TPU v7x, 256 devices: a whole 4x4x8 slice. The times are simulated.
256 devices in a mesh: seq: 64 (over z, y, core), tensor: 4 (over x).
Axes of the slice: x: 4, y: 4, z: 8, core: 2. Of those that a mesh axis runs over, the one named last changes fastest.
Arguments:
- byte_rows: bfloat16 [32768, 1024], P('seq'), may hold values from -6 to 6
- patch_lengths: int32 [64, 128], P('seq'), may hold values from 1 to 16, 512 in all within a row
- pool_query: bfloat16 [1024, 1024], P(None, 'tensor')
- pool_key: bfloat16 [1024, 1024], P(None, 'tensor')
- pool_value: bfloat16 [1024, 1024], P(None, 'tensor'), may hold values from -0.1875 to 0.1875
- pool_out: bfloat16 [1024, 4096], P('tensor'), may hold values from -0.1875 to 0.1875
- norm_gain: bfloat16 [4096], replicated, may hold values from 0.5 to 1.5
- query_weight: bfloat16 [4096, 2048], P('seq', 'tensor')
- key_weight: bfloat16 [4096, 512], P(None, 'tensor')
- value_weight: bfloat16 [4096, 512], P(None, 'tensor'), may hold values from -0.09375 to 0.09375
- out_weight: bfloat16 [2048, 4096], P('tensor'), may hold values from -0.125 to 0.125
- cotangent: bfloat16 [8192, 4096], P(('seq', 'tensor')), may hold values from -6 to 6
Outputs:
- layer_out: bfloat16 [8192, 4096], P(('seq', 'tensor'))
- patch_grad: bfloat16 [8192, 4096], P(('seq', 'tensor'))
Inputs may be any that keep to these rules, and one draw needn't show every extreme that they name: `patch_lengths`: every patch holds at least one byte.
All inputs are finite; a program needn't handle non-finite values.
Results may differ from a plain program's by a relative error of at most 0.03.
Values may be sent and summed in bfloat16 or wider, within the bound.
A program may use at most 128 MiB of HBM per device.

v0:
```python
import jax
import jax.numpy as jnp
from jax import lax
from jax.sharding import PartitionSpec as P

EPS = 1e-05
NEG = -1e30


def pool_group(byte_block, lengths, pool_query, pool_key, pool_value, pool_out, head_size):
    ends = jnp.cumsum(lengths)
    starts = ends - lengths
    where_at = jnp.arange(byte_block.shape[0], dtype=jnp.int32)
    member = (where_at[None, :] >= starts[:, None]) & (where_at[None, :] < ends[:, None])
    sums = jnp.dot(member.astype(jnp.bfloat16), byte_block, preferred_element_type=jnp.float32)
    means = (sums / lengths[:, None].astype(jnp.float32)).astype(jnp.bfloat16)
    pool_q = jnp.dot(means, pool_query, preferred_element_type=jnp.float32).astype(jnp.bfloat16)
    pool_k = jnp.dot(byte_block, pool_key, preferred_element_type=jnp.float32).astype(jnp.bfloat16)
    pool_v = jnp.dot(byte_block, pool_value, preferred_element_type=jnp.float32).astype(
        jnp.bfloat16
    )
    heads = pool_query.shape[1] // head_size
    q_heads = pool_q.reshape(-1, heads, head_size)
    k_heads = pool_k.reshape(-1, heads, head_size)
    v_heads = pool_v.reshape(-1, heads, head_size)
    scores = jnp.einsum(
        "phd,bhd->hpb", q_heads, k_heads, preferred_element_type=jnp.float32
    ) * head_size ** (-0.5)
    scores = jnp.where(member[None], scores, NEG)
    top = jnp.max(scores, -1, keepdims=True)
    expo = jnp.exp(scores - top)
    weights = (expo / jnp.sum(expo, -1, keepdims=True)).astype(jnp.bfloat16)
    pooled = jnp.einsum("hpb,bhd->phd", weights, v_heads, preferred_element_type=jnp.float32)
    pooled = pooled.reshape(lengths.shape[0], -1).astype(jnp.bfloat16)
    return jnp.dot(pooled, pool_out, preferred_element_type=jnp.float32)


def head_scores(q_heads, key_block, q_pos, key_pos):
    scale = q_heads.shape[-1] ** (-0.5)
    scores = (
        jnp.einsum("gqd,kd->gqk", q_heads, key_block, preferred_element_type=jnp.float32) * scale
    )
    return jnp.where(key_pos[None, None, :] <= q_pos[None, :, None], scores, NEG)


def key_terms(q_heads, g_heads, lse, delta, q_pos, key_block, value_block, key_pos):
    scores = head_scores(q_heads, key_block, q_pos, key_pos)
    prob = jnp.exp(scores - lse[..., None])
    weights = prob.astype(jnp.bfloat16)
    dprob = jnp.einsum("gqd,kd->gqk", g_heads, value_block, preferred_element_type=jnp.float32)
    dscore = (prob * (dprob - delta[..., None])).astype(jnp.bfloat16)
    scale = q_heads.shape[-1] ** (-0.5)
    grad_k = jnp.einsum("gqk,gqd->kd", dscore, q_heads, preferred_element_type=jnp.float32) * scale
    grad_v = jnp.einsum("gqk,gqd->kd", weights, g_heads, preferred_element_type=jnp.float32)
    return (grad_k, grad_v)


def block_size(count, unit_rows):
    units = count // unit_rows
    width = 1
    while width < 8 and units % (width * 2) == 0:
        width = width * 2
    return unit_rows * width


def split_heads(rows_array, group, head_size):
    return rows_array.reshape(rows_array.shape[0], group, head_size).transpose(1, 0, 2)


def on_device(
    byte_rows,
    patch_lengths,
    pool_query,
    pool_key,
    pool_value,
    pool_out,
    norm_gain,
    query_weight,
    key_weight,
    value_weight,
    out_weight,
    cotangent,
):
    head_size = key_weight.shape[1]
    partial_value = pool_group(
        byte_rows, patch_lengths[0], pool_query, pool_key, pool_value, pool_out, head_size
    )
    patches = lax.psum_scatter(partial_value, "tensor", scatter_dimension=0, tiled=True).astype(
        jnp.bfloat16
    )
    hidden = patches.astype(jnp.float32)
    inv = lax.rsqrt(jnp.mean(hidden * hidden, -1, keepdims=True) + EPS)
    unit = hidden * inv
    gain = norm_gain.astype(jnp.float32)
    normed = (unit * gain).astype(jnp.bfloat16)
    normed_all, grad_rows = (
        lax.all_gather(normed, "tensor", axis=0, tiled=True),
        lax.all_gather(cotangent, "tensor", axis=0, tiled=True),
    )
    query_full = lax.all_gather(query_weight, "seq", axis=0, tiled=True)
    queries = jnp.dot(normed_all, query_full, preferred_element_type=jnp.float32).astype(
        jnp.bfloat16
    )
    keys = jnp.dot(normed_all, key_weight, preferred_element_type=jnp.float32).astype(jnp.bfloat16)
    values = jnp.dot(normed_all, value_weight, preferred_element_type=jnp.float32).astype(
        jnp.bfloat16
    )
    keys_all, values_all = (
        lax.all_gather(keys, "seq", axis=0, tiled=True),
        lax.all_gather(values, "seq", axis=0, tiled=True),
    )
    rows = queries.shape[0]
    group = queries.shape[1] // head_size
    first = lax.axis_index("seq") * rows
    q_pos = first + jnp.arange(rows, dtype=jnp.int32)
    q_heads = split_heads(queries, group, head_size)
    total = keys_all.shape[0]
    block = min(total, 1024)
    count = total // block

    def key_block(index):
        start = index * block
        kb = lax.dynamic_slice_in_dim(keys_all, start, block, 0)
        vb = lax.dynamic_slice_in_dim(values_all, start, block, 0)
        return (kb, vb, start + jnp.arange(block, dtype=jnp.int32))

    def max_pass(index, carry):
        top, mass = carry
        kb, vb, key_pos = key_block(index)
        scores = head_scores(q_heads, kb, q_pos, key_pos)
        new_top = jnp.maximum(top, jnp.max(scores, -1))
        mass = mass * jnp.exp(top - new_top) + jnp.sum(jnp.exp(scores - new_top[..., None]), -1)
        return (new_top, mass)

    start_top = jnp.full((group, rows), NEG, jnp.float32)
    top, mass = lax.fori_loop(
        0, count, max_pass, (start_top, jnp.zeros((group, rows), jnp.float32))
    )
    lse = top + jnp.log(mass)

    def value_pass(index, acc):
        kb, vb, key_pos = key_block(index)
        scores = head_scores(q_heads, kb, q_pos, key_pos)
        weights = jnp.exp(scores - lse[..., None]).astype(jnp.bfloat16)
        return acc + jnp.einsum("gqk,kd->gqd", weights, vb, preferred_element_type=jnp.float32)

    acc = lax.fori_loop(0, count, value_pass, jnp.zeros((group, rows, head_size), jnp.float32))
    attn = acc.transpose(1, 0, 2).reshape(rows, group * head_size).astype(jnp.bfloat16)
    out_part = jnp.dot(attn, out_weight, preferred_element_type=jnp.float32)
    grad_attn = lax.dot_general(
        grad_rows, out_weight, (((1,), (1,)), ((), ())), preferred_element_type=jnp.float32
    ).astype(jnp.bfloat16)
    g_heads = split_heads(grad_attn, group, head_size)
    o_heads = split_heads(attn, group, head_size)
    delta = jnp.sum(g_heads.astype(jnp.float32) * o_heads.astype(jnp.float32), -1)

    def grad_pass(index, grad_acc):
        kb, vb, key_pos = key_block(index)
        scores = head_scores(q_heads, kb, q_pos, key_pos)
        prob = jnp.exp(scores - lse[..., None])
        dprob = jnp.einsum("gqd,kd->gqk", g_heads, vb, preferred_element_type=jnp.float32)
        dscore = (prob * (dprob - delta[..., None])).astype(jnp.bfloat16)
        return grad_acc + jnp.einsum("gqk,kd->gqd", dscore, kb, preferred_element_type=jnp.float32)

    grad_acc = lax.fori_loop(0, count, grad_pass, jnp.zeros((group, rows, head_size), jnp.float32))
    grad_q = (
        (grad_acc * head_size ** (-0.5))
        .transpose(1, 0, 2)
        .reshape(rows, group * head_size)
        .astype(jnp.bfloat16)
    )
    lse_all, delta_all = (
        lax.all_gather(lse, "seq", axis=1, tiled=True),
        lax.all_gather(delta, "seq", axis=1, tiled=True),
    )
    empty = jnp.zeros((rows, head_size), jnp.float32)
    q_piece = lax.all_gather(queries, "seq", axis=0, tiled=True)
    g_piece = lax.all_gather(grad_attn, "seq", axis=0, tiled=True)
    length = q_piece.shape[0]
    sub = block_size(length, rows)

    def step(inner, index):
        at = index * sub
        q_rows = lax.dynamic_slice_in_dim(q_piece, at, sub, 0)
        g_rows = lax.dynamic_slice_in_dim(g_piece, at, sub, 0)
        lse_rows = lax.dynamic_slice_in_dim(lse_all, at, sub, 1)
        delta_rows = lax.dynamic_slice_in_dim(delta_all, at, sub, 1)
        pos_rows = at + jnp.arange(sub, dtype=jnp.int32)
        grad_k, grad_v = key_terms(
            split_heads(q_rows, group, head_size),
            split_heads(g_rows, group, head_size),
            lse_rows,
            delta_rows,
            pos_rows,
            keys,
            values,
            q_pos,
        )
        return ((inner[0] + grad_k, inner[1] + grad_v), None)

    result, unused = lax.scan(step, (empty, empty), jnp.arange(length // sub, dtype=jnp.int32))
    sum_k, sum_v = result
    grad_k = sum_k.astype(jnp.bfloat16)
    grad_v = sum_v.astype(jnp.bfloat16)
    contract = (((1,), (1,)), ((), ()))
    grad_part = lax.dot_general(grad_q, query_full, contract, preferred_element_type=jnp.float32)
    grad_part = grad_part + lax.dot_general(
        grad_k, key_weight, contract, preferred_element_type=jnp.float32
    )
    grad_part = grad_part + lax.dot_general(
        grad_v, value_weight, contract, preferred_element_type=jnp.float32
    )
    layer_part, grad_normed = (
        lax.psum_scatter(
            out_part.astype(jnp.bfloat16), "tensor", scatter_dimension=0, tiled=True
        ).astype(jnp.float32),
        lax.psum_scatter(
            grad_part.astype(jnp.bfloat16), "tensor", scatter_dimension=0, tiled=True
        ).astype(jnp.float32),
    )
    layer_out = (hidden + layer_part).astype(jnp.bfloat16)
    scaled = grad_normed * gain
    patch_grad = cotangent.astype(jnp.float32) + inv * (
        scaled - unit * jnp.mean(scaled * unit, -1, keepdims=True)
    )
    return (layer_out, patch_grad.astype(jnp.bfloat16))


def solution(mesh):
    placed = (
        P("seq", None),
        P("seq", None),
        P(None, "tensor"),
        P(None, "tensor"),
        P(None, "tensor"),
        P("tensor", None),
        P(),
        P("seq", "tensor"),
        P(None, "tensor"),
        P(None, "tensor"),
        P("tensor", None),
        P(("seq", "tensor"), None),
    )
    return jax.shard_map(
        on_device,
        mesh=mesh,
        in_specs=placed,
        out_specs=(P(("seq", "tensor"), None), P(("seq", "tensor"), None)),
        check_vma=False,
    )
```

profile of v0, /device:TPU:2, one launch (start us, length us, event | category | flops | bytes accessed | tf_op | source)
XLA Modules:
  0.0 753.6 jit_solution(12896114840389394539)
XLA Ops:
  20.7 33.4 %reduce-scatter.4.cloned.1.call-done = f32[32,4096]{1,0:T(8,128)} async-done(((f32[128,4096]{1,0:T(8,128)}), f32[32,4096]{1,0:T(8,128)}) %reduce-scatter.4.cloned.1.call-update) | async-done | bytes 524304 | tf_op jit(solution)/shard_map/reduce_scatter | solution.py:88
  57.6 25.7 %all-gather.8.cloned.1.call-done = bf16[128,4096]{1,0:T(8,128)(2,1)} async-done(((bf16[32,4096]{1,0:T(8,128)(2,1)}), bf16[128,4096]{1,0:T(8,128)(2,1)}) %all-gather.8.cloned.1.call-update) | async-done | bytes 1048592 | tf_op jit(solution)/shard_map/all_gather | solution.py:97
  88.4 23.8 %all-gather.16.cloned.1.call-done = bf16[128,4096]{1,0:T(8,128)(2,1)} async-done(((bf16[32,4096]{1,0:T(8,128)(2,1)}), bf16[128,4096]{1,0:T(8,128)(2,1)}) %all-gather.16.cloned.1.call-update) | async-done | bytes 1048592 | tf_op jit(solution)/shard_map/all_gather | solution.py:98
  112.1 4.7 convolution_convert_fusion.3
  120.3 75.2 %all-gather.12.cloned.1.call-done = bf16[4096,512]{1,0:T(8,128)(2,1)} async-done(((bf16[64,512]{1,0:T(8,128)(2,1)}), bf16[4096,512]{1,0:T(8,128)(2,1)}) %all-gather.12.cloned.1.call-update) | async-done | bytes 4194320 | tf_op jit(solution)/shard_map/all_gather | solution.py:100
  195.5 3.6 convolution_convert_fusion.4
  200.0 73.0 %all-gather.10.cloned.1.call-done = bf16[8192,128]{1,0:T(8,128)(2,1)} async-done(((bf16[128,128]{1,0:T(8,128)(2,1)}), bf16[8192,128]{1,0:T(8,128)(2,1)}) %all-gather.10.cloned.1.call-update) | async-done | bytes 2097168 | tf_op jit(solution)/shard_map/all_gather | solution.py:109
  273.0 40.9 %while.57 = (s32[]{:T(128)}, f32[4,128]{1,0:T(4,128)S(1)}, f32[4,128]{1,0:T(4,128)S(1)}, bf16[8192,128]{1,0:T(8,128)(2,1)}, bf16[4,128,128]{2,1,0:T(8,128)(2,1)S...) while((s32[]{:T(128)}, f32[4,128]{1,0:T(4,128)S(1)}, ...), condition=%wide.region_8.9_spmd.clone, body=%wide.region_5.8_spmd.clone.sunk | while | flops 138022528 | bytes 5016754 | solution.py:136
  314.0 37.1 %all-gather.14.cloned.1.call-done = bf16[8192,128]{1,0:T(8,128)(2,1)} async-done(((bf16[128,128]{1,0:T(8,128)(2,1)}), bf16[8192,128]{1,0:T(8,128)(2,1)}) %all-gather.14.cloned.1.call-update) | async-done | bytes 2097168 | tf_op jit(solution)/shard_map/all_gather | solution.py:110
  351.1 17.8 %while.58 = (s32[]{:T(128)}, f32[4,128,128]{2,1,0:T(8,128)S(1)}, bf16[8192,128]{1,0:T(8,128)(2,1)}, bf16[4,128,128]{2,1,0:T(8,128)(2,1)S(1)}, f32[4,128]{1,0:T(4...) while((s32[]{:T(128)}, f32[4,128,128]{2,1,0:T(8,128)S(1)}, ...), condition=%wide.region_10.11_spmd.clone, body=%wide.region_9.10_spmd.clone.sunk | while | flops 270795904 | bytes 1454772 | solution.py:147
  369.7 46.0 %while.59 = (s32[]{:T(128)}, f32[4,128,128]{2,1,0:T(8,128)S(1)}, bf16[8192,128]{1,0:T(8,128)(2,1)}, bf16[4,128,128]{2,1,0:T(8,128)(2,1)S(1)}, f32[4,128]{1,0:T(4...) while((s32[]{:T(128)}, f32[4,128,128]{2,1,0:T(8,128)S(1)}, ...), condition=%wide.region_14.15_spmd.clone, body=%wide.region_13.14_spmd.clone.sunk | while | flops 406062208 | bytes 6568676 | solution.py:165
  415.9 52.1 %all_gather.33 = f32[4,8192]{1,0:T(4,128)} all-gather(f32[4,128]{1,0:T(4,128)S(1)} %get-tuple-element.1079), channel_id=1, replica_groups=mesh['seq'=64,'tensor'=4] {'seq'}, dimensions={1}, use_global_device_ids=true | all-gather | bytes 133120 | tf_op jit(solution)/shard_map/all_gather | solution.py:173
  468.0 52.3 %all_gather.35 = f32[4,8192]{1,0:T(4,128)} all-gather(f32[4,128]{1,0:T(4,128)S(1)} %get-tuple-element.1077), channel_id=1, replica_groups=mesh['seq'=64,'tensor'=4] {'seq'}, dimensions={1}, use_global_device_ids=true | all-gather | bytes 133120 | tf_op jit(solution)/shard_map/all_gather | solution.py:174
  520.3 5.0 fusion.109
  525.9 164.2 %while.60 = (s32[]{:T(128)}, f32[128,128]{1,0:T(8,128)S(1)}, f32[128,128]{1,0:T(8,128)S(1)}, s32[8]{0:T(128)}, bf16[8192,512]{1,0:T(8,128)(2,1)}, /*index=5*/bf1...) while((s32[]{:T(128)}, f32[128,128]{1,0:T(8,128)S(1)}, ...), condition=%wide.region_16.17_spmd.clone, body=%wide.region_15.16_spmd.clone.sunk | while | flops 540755072 | bytes 27960580 | solution.py:201
  540.9 3.3 fusion.185
  561.4 3.3 fusion.185
  582.0 3.3 fusion.185
  602.5 3.3 fusion.185
  623.0 3.3 fusion.185
  643.6 3.3 fusion.185
  694.1 4.0 convolution_convert_fusion
  698.1 18.3 %reduce-scatter.8.cloned.1.call-done = bf16[32,4096]{1,0:T(8,128)(2,1)} async-done(((bf16[128,4096]{1,0:T(8,128)(2,1)}), bf16[32,4096]{1,0:T(8,128)(2,1)}) %reduce-scatter.8.cloned.1.call-update) | async-done | bytes 262160 | tf_op jit(solution)/shard_map/reduce_scatter | solution.py:217
  717.6 27.1 %reduce-scatter.6.cloned.1.call-done = bf16[32,4096]{1,0:T(8,128)(2,1)} async-done(((bf16[128,4096]{1,0:T(8,128)(2,1)}), bf16[32,4096]{1,0:T(8,128)(2,1)}) %reduce-scatter.6.cloned.1.call-update) | async-done | bytes 262160 | tf_op jit(solution)/shard_map/reduce_scatter | solution.py:214
  (357 shorter events, 276.8 us)
Async XLA Ops:
  7.2 11.0 %copy-start = (bf16[256,4096]{1,0:T(8,128)(2,1)S(1)}, bf16[256,4096]{1,0:T(8,128)(2,1)}, u32[]{:S(2)}) copy-start(bf16[256,4096]{1,0:T(8,128)(2,1)} %param.25) | copy-start | bytes 6291460
  7.2 47.0 %reduce-scatter.4.cloned.1.call-start = ((), (), s32[]{:S(2)}) async-start(), calls=%async_computation.3 | async-start | bytes 2621440 | tf_op jit(solution)/shard_map/reduce_scatter | solution.py:88
  20.0 63.2 %all-gather.8.cloned.1.call-start = ((), (), s32[]{:S(2)}) async-start(), calls=%async_computation.4 | async-start | bytes 1310720 | tf_op jit(solution)/shard_map/all_gather | solution.py:97
  20.7 36.9 %copy-start.9 = (f32[4096]{0:T(1024)}, f32[4096]{0:T(1024)S(1)}, u32[]{:S(2)}) copy-start(f32[4096]{0:T(1024)S(1)} %convert_element_type.141) | copy-start | bytes 49156
  56.2 55.9 %all-gather.16.cloned.1.call-start = ((), (), s32[]{:S(2)}) async-start(), calls=%async_computation.9 | async-start | bytes 1310720 | tf_op jit(solution)/shard_map/all_gather | solution.py:98
  57.0 138.5 %all-gather.12.cloned.1.call-start = ((), (), s32[]{:S(2)}) async-start(), calls=%async_computation.6 | async-start | bytes 4259840 | tf_op jit(solution)/shard_map/all_gather | solution.py:100
  57.5 215.5 %all-gather.10.cloned.1.call-start = ((), (), s32[]{:S(2)}) async-start(), calls=%async_computation.5 | async-start | bytes 2129920 | tf_op jit(solution)/shard_map/all_gather | solution.py:109
  86.0 265.1 %all-gather.14.cloned.1.call-start = ((), (), s32[]{:S(2)}) async-start(), calls=%async_computation.7 | async-start | bytes 2129920 | tf_op jit(solution)/shard_map/all_gather | solution.py:110
  88.3 437.0 %all-gather.20.cloned.1.call-start = ((), (), s32[]{:S(2)}) async-start(), calls=%async_computation.11 | async-start | bytes 8519680 | tf_op jit(solution)/shard_map/all_gather | solution.py:178
  116.9 408.5 %all-gather.18.cloned.1.call-start = ((), (), s32[]{:S(2)}) async-start(), calls=%async_computation.10 | async-start | bytes 8519680 | tf_op jit(solution)/shard_map/all_gather | solution.py:177
  200.0 516.5 %reduce-scatter.8.cloned.1.call-start = ((), (), s32[]{:S(2)}) async-start(), calls=%async_computation.12 | async-start | bytes 1310720 | tf_op jit(solution)/shard_map/reduce_scatter | solution.py:217
  273.0 78.0 %copy-start.11 = (f32[4,128,128]{2,1,0:T(8,128)S(1)}, f32[4,128,128]{2,1,0:T(8,128)}, u32[]{:S(2)}) copy-start(f32[4,128,128]{2,1,0:T(8,128)} %custom-call.2) | copy-start | bytes 786436
  351.1 18.0 %copy-start.5 = (bf16[128,512]{0,1:T(8,128)(2,1)S(1)}, bf16[128,512]{0,1:T(8,128)(2,1)}, u32[]{:S(2)}) copy-start(bf16[128,512]{0,1:T(8,128)(2,1)} %copy.38) | copy-start | bytes 393220
  351.1 18.0 %copy-start.12 = (f32[4,128,128]{2,1,0:T(8,128)S(1)}, f32[4,128,128]{2,1,0:T(8,128)}, u32[]{:S(2)}) copy-start(f32[4,128,128]{2,1,0:T(8,128)} %custom-call.3) | copy-start | bytes 786436
  553.9 6.0 copy-start.1
  574.4 6.0 copy-start.1
  594.9 6.0 copy-start.1
  615.5 6.0 copy-start.1
  636.0 6.0 copy-start.1
  656.5 6.0 copy-start.1
  694.0 50.7 %reduce-scatter.6.cloned.1.call-start = ((), (), s32[]{:S(2)}) async-start(), calls=%async_computation.8 | async-start | bytes 1310720 | tf_op jit(solution)/shard_map/reduce_scatter | solution.py:214
  694.1 22.4 %copy-start.10 = (f32[4096]{0:T(1024)S(1)}, f32[4096]{0:T(1024)}, u32[]{:S(2)}) copy-start(f32[4096]{0:T(1024)} %copy-done.9) | copy-start | bytes 49156
  694.1 22.4 %copy-start.16 = (f32[32]{0:T(128)S(1)}, f32[32]{0:T(128)}, u32[]{:S(2)}) copy-start(f32[32]{0:T(128)} %copy-done.15) | copy-start | bytes 388
  694.1 50.6 %copy-start.8 = (bf16[32,4096]{1,0:T(8,128)(2,1)S(1)}, bf16[32,4096]{1,0:T(8,128)(2,1)}, u32[]{:S(2)}) copy-start(bf16[32,4096]{1,0:T(8,128)(2,1)} %param.31) | copy-start | bytes 786436
  (17 other events, 50.7 us)
Sparse Core Ops, SparseCore 0:
  20.2 33.9 reduce-scatter.3
  56.7 26.5 all-gather.7
  85.2 26.8 all-gather.15
  115.1 80.2 all-gather.11
  198.5 74.5 all-gather.9
  276.0 74.9 all-gather.13
  354.2 80.7 all-gather.19
  438.1 80.2 all-gather.17
  694.1 22.2 reduce-scatter.7
  718.8 25.8 reduce-scatter.5
where the time goes:
time: 759 us; the launch traced here: 754 us
  waiting for transfers between devices  315 us (42%)
  matrix products  183 us (24%)
  blocking collectives  104 us (14%)
  local copies, waits for them, and re-layouts  99.3 us (13%)
  other arithmetic  29.6 us (4%)
  between operations  14.5 us (2%)
    all_gather x1, waiting for transfers between devices, on_device(): query_full = lax.all_gather(query_weight, 'seq', axis=0, tiled=True)  75.2 us
    all_gather x1, waiting for transfers between devices, on_device(): lax.all_gather(keys, 'seq', axis=0, tiled=True)  73 us
    dot_general x24, matrix products, head_scores(): jnp.einsum('gqd,kd->gqk', q_heads, key_block, preferred_element_type=jnp....  65.8 us
    all_gather x1, blocking collectives, on_device(): lax.all_gather(delta, 'seq', axis=1, tiled=True)  52.3 us
    all_gather x1, blocking collectives, on_device(): lax.all_gather(lse, 'seq', axis=1, tiled=True)  52.1 us
    dynamic_slice x16, local copies, waits for them, and re-layouts, step(): g_rows = lax.dynamic_slice_in_dim(g_piece, at, sub, 0)  39.2 us
    all_gather x1, waiting for transfers between devices, on_device(): lax.all_gather(values, 'seq', axis=0, tiled=True)  37.1 us
    reduce_scatter x1, waiting for transfers between devices, on_device(): lax.psum_scatter(partial_value, 'tensor', scatter_dimension=0, tiled=True)  33.4 us
  transfers between devices with their start and end apart: 10, of which 8 were waited for; matrix products, arithmetic and copies ran while one was open for 17% of the time, Pallas kernels for 0%

commit v1 on v0

v1 whole, which is shorter than its diff:
```python
import math

import jax
import jax.numpy as jnp
from jax import lax
from jax.experimental import pallas as pl
from jax.experimental.pallas import tpu as pltpu
from jax.sharding import PartitionSpec as P

EPS = 1e-05
NEG = -1e30
MESH = pl.DeviceIdType.MESH
NZ, NY, NX = 8, 4, 4
HD = 128
GROUP = 4
ROWS = 128
HALF = 64
SHARDS = 64
D = 4096
OWN = 32
KB = 512
VMEM = 56 * 1024 * 1024
F32 = jnp.float32
BF16 = jnp.bfloat16
NT = (((1,), (1,)), ((), ()))
TN = (((0,), (0,)), ((), ()))


def mm(a, b):
    return jnp.dot(a, b, preferred_element_type=F32)


def dg(a, b, dims):
    return lax.dot_general(a, b, dims, preferred_element_type=F32)


class Place:
    def __init__(self):
        s = lax.axis_index("seq")
        self.s = s
        self.z = lax.div(s, 8)
        self.y = lax.rem(lax.div(s, 2), 4)
        self.c = lax.rem(s, 2)
        self.t = lax.axis_index("tensor")
        self.sib = self.seq(self.z, self.y, 1 - self.c)
        self.up = self.seq(self.zz(1), self.y, self.c)
        self.down = self.seq(self.zz(-1), self.y, self.c)
        self.north = self.seq(self.z, self.yy(1), self.c)
        self.south = self.seq(self.z, self.yy(-1), self.c)
        self.twin = SHARDS - 1 - s

    def zz(self, i):
        return lax.rem(self.z + NZ + i, NZ)

    def yy(self, i):
        return lax.rem(self.y + NY + i, NY)

    def tt(self, i):
        return lax.rem(self.t + NX + i, NX)

    def seq(self, z, y, c):
        return (z * NY + y) * 2 + c


class Net:
    def __init__(self, send, recv):
        self.send, self.recv, self.all = send, recv, []

    def put(self, src, dst, **device):
        n = len(self.all)
        copy = pltpu.make_async_remote_copy(
            src_ref=src,
            dst_ref=dst,
            send_sem=self.send.at[n],
            recv_sem=self.recv.at[n],
            device_id=device,
            device_id_type=MESH,
        )
        copy.start()
        self.all.append(copy)
        return copy

    def finish(self):
        for copy in self.all:
            copy.wait_send()


def greet(devices):
    barrier = pltpu.get_barrier_semaphore()
    for device in devices:
        pl.semaphore_signal(barrier, inc=1, device_id=device, device_id_type=MESH)
    pl.semaphore_wait(barrier, len(devices))


def ring_partners(at):
    return [{"seq": d} for d in (at.sib, at.up, at.down, at.north, at.south)]


def line_partners(at):
    return [{"tensor": at.tt(1)}, {"tensor": at.tt(-1)}]


def run(chains):
    chains = list(chains)
    while chains:
        left = []
        for chain in chains:
            try:
                next(chain)
                left.append(chain)
            except StopIteration:
                pass
        chains = left


def same(net, view, **device):
    return net.put(view, view, **device)


def gather_zy(net, at, buf):
    rows = buf.shape[4] // 2
    zz, yy, c, y = at.zz, at.yy, at.c, at.y
    for i in range(1, 4):
        p = same(net, buf.at[zz(1 - i), y, c, 0], seq=at.up)
        m = same(net, buf.at[zz(i - 1), y, c, 0], seq=at.down)
        yield
        p.wait_recv()
        m.wait_recv()
    p = same(net, buf.at[zz(-3), y, c, 0, pl.ds(0, rows)], seq=at.up)
    m = same(net, buf.at[zz(3), y, c, 0, pl.ds(rows, rows)], seq=at.down)
    yield
    p.wait_recv()
    m.wait_recv()
    every = pl.ds(0, NZ)
    p = same(net, buf.at[every, y, c, 0], seq=at.north)
    m = same(net, buf.at[every, y, c, 0], seq=at.south)
    sib = [same(net, buf.at[every, y, c, 0], seq=at.sib)]
    yield
    p.wait_recv()
    m.wait_recv()
    p = same(net, buf.at[pl.ds(0, 4), yy(-1), c, 0], seq=at.north)
    m = same(net, buf.at[pl.ds(4, 4), yy(1), c, 0], seq=at.south)
    sib.append(same(net, buf.at[every, yy(-1), c, 0], seq=at.sib))
    sib.append(same(net, buf.at[every, yy(1), c, 0], seq=at.sib))
    yield
    p.wait_recv()
    m.wait_recv()
    sib.append(same(net, buf.at[every, yy(2), c, 0], seq=at.sib))
    yield
    for copy in sib:
        copy.wait_recv()


def gather_yz(net, at, buf):
    rows = buf.shape[4] // 2
    zz, yy, c, z = at.zz, at.yy, at.c, at.z
    p = same(net, buf.at[z, at.y, c, 1], seq=at.north)
    m = same(net, buf.at[z, at.y, c, 1], seq=at.south)
    yield
    p.wait_recv()
    m.wait_recv()
    p = same(net, buf.at[z, yy(-1), c, 1, pl.ds(0, rows)], seq=at.north)
    m = same(net, buf.at[z, yy(1), c, 1, pl.ds(rows, rows)], seq=at.south)
    yield
    p.wait_recv()
    m.wait_recv()
    every = pl.ds(0, NY)
    sib = [same(net, buf.at[z, every, c, 1], seq=at.sib)]
    for i in range(1, 4):
        p = same(net, buf.at[zz(1 - i), every, c, 1], seq=at.up)
        m = same(net, buf.at[zz(i - 1), every, c, 1], seq=at.down)
        yield
        p.wait_recv()
        m.wait_recv()
        sib.append(same(net, buf.at[zz(-i), every, c, 1], seq=at.sib))
        sib.append(same(net, buf.at[zz(i), every, c, 1], seq=at.sib))
    p = same(net, buf.at[zz(-3), pl.ds(0, 2), c, 1], seq=at.up)
    m = same(net, buf.at[zz(3), pl.ds(2, 2), c, 1], seq=at.down)
    yield
    p.wait_recv()
    m.wait_recv()
    sib.append(same(net, buf.at[zz(4), every, c, 1], seq=at.sib))
    yield
    for copy in sib:
        copy.wait_recv()


def gather_x(net, at, buf):
    rows = buf.shape[1] // 2
    tt = at.tt
    p = same(net, buf.at[at.t], tensor=tt(1))
    m = same(net, buf.at[at.t], tensor=tt(-1))
    yield
    p.wait_recv()
    m.wait_recv()
    p = same(net, buf.at[tt(-1), pl.ds(0, rows)], tensor=tt(1))
    m = same(net, buf.at[tt(1), pl.ds(rows, rows)], tensor=tt(-1))
    yield
    p.wait_recv()
    m.wait_recv()


def add_into(ref, other):
    ref[...] = (ref[...].astype(F32) + other[...].astype(F32)).astype(BF16)


def scatter_x(net, at, part, first, second, result):
    rows = part.shape[1] // 2
    tt = at.tt
    low, high = pl.ds(0, rows), pl.ds(rows, rows)
    p = net.put(part.at[tt(2), low], first.at[0], tensor=tt(1))
    m = net.put(part.at[tt(2), high], first.at[1], tensor=tt(-1))
    yield
    p.wait_recv()
    m.wait_recv()
    add_into(part.at[tt(1), low], first.at[0])
    add_into(part.at[tt(-1), high], first.at[1])
    p = net.put(part.at[tt(1)], second.at[0], tensor=tt(1))
    m = net.put(part.at[tt(-1)], second.at[1], tensor=tt(-1))
    yield
    p.wait_recv()
    m.wait_recv()
    result(part[at.t].astype(F32) + second[0].astype(F32) + second[1].astype(F32))


def scatter_yz(net, at, acc, y_first, y_second, z_first, z_next, out):
    yy, zz = at.yy, at.zz
    low, high = pl.ds(0, 4), pl.ds(4, 4)
    p = net.put(acc.at[yy(2), low], y_first.at[0], seq=at.north)
    m = net.put(acc.at[yy(2), high], y_first.at[1], seq=at.south)
    yield
    p.wait_recv()
    m.wait_recv()
    add_into(acc.at[yy(1), low], y_first.at[0])
    p = net.put(acc.at[yy(1)], y_second.at[0], seq=at.north)
    add_into(acc.at[yy(-1), high], y_first.at[1])
    m = net.put(acc.at[yy(-1)], y_second.at[1], seq=at.south)
    yield
    p.wait_recv()
    m.wait_recv()
    add_into(acc.at[at.y], y_second.at[0])
    add_into(acc.at[at.y], y_second.at[1])
    yield from scatter_line(net, acc.at[at.y], zz, at.up, at.down, z_first, z_next, out, ROWS // 2)


def scatter_zy(net, at, acc, z_first, z_next, y_first, y_second, out):
    yy = at.yy
    mine = acc.at[at.z]
    yield from scatter_line(net, acc, at.zz, at.up, at.down, z_first, z_next, None, NY // 2)
    low, high = pl.ds(0, ROWS // 2), pl.ds(ROWS // 2, ROWS // 2)
    p = net.put(mine.at[yy(2), low], y_first.at[0], seq=at.north)
    m = net.put(mine.at[yy(2), high], y_first.at[1], seq=at.south)
    yield
    p.wait_recv()
    m.wait_recv()
    add_into(mine.at[yy(1), low], y_first.at[0])
    add_into(mine.at[yy(-1), high], y_first.at[1])
    p = net.put(mine.at[yy(1)], y_second.at[0], seq=at.north)
    m = net.put(mine.at[yy(-1)], y_second.at[1], seq=at.south)
    yield
    p.wait_recv()
    m.wait_recv()
    out[...] = (
        mine[at.y].astype(F32) + y_second[0].astype(F32) + y_second[1].astype(F32)
    ).astype(BF16)


def scatter_line(net, acc, zz, up, down, z_first, z_next, out, cut):
    low, high = pl.ds(0, cut), pl.ds(cut, cut)
    p = net.put(acc.at[zz(4), low], z_first.at[0], seq=up)
    m = net.put(acc.at[zz(4), high], z_first.at[1], seq=down)
    yield
    p.wait_recv()
    m.wait_recv()
    add_into(acc.at[zz(3), low], z_first.at[0])
    add_into(acc.at[zz(-3), high], z_first.at[1])
    for i in (3, 2, 1):
        p = net.put(acc.at[zz(i)], z_next.at[i - 1, 0], seq=up)
        m = net.put(acc.at[zz(-i)], z_next.at[i - 1, 1], seq=down)
        yield
        p.wait_recv()
        m.wait_recv()
        if i > 1:
            add_into(acc.at[zz(i - 1)], z_next.at[i - 1, 0])
            add_into(acc.at[zz(1 - i)], z_next.at[i - 1, 1])
    total = acc[zz(0)].astype(F32) + z_next[0, 0].astype(F32) + z_next[0, 1].astype(F32)
    if out is None:
        acc[zz(0)] = total.astype(BF16)
    else:
        out[...] = total.astype(BF16)


def front_kernel(
    pooled, pool_out, gain, cot, wq, wk, wv, wo,
    q, g, kv, patches, wq_all,
    part, normed, cots, first, second, acc, wk_v, wv_v, wo_v, send, recv, local,
):
    at = Place()
    net = Net(send, recv)
    loads = [
        pltpu.make_async_copy(src, dst, local.at[i])
        for i, (src, dst) in enumerate(((wk, wk_v), (wv, wv_v), (wo, wo_v)))
    ]
    for load in loads:
        load.start()
    cots[at.t] = cot[...]
    wq_all[at.z, at.y, at.c] = wq[...].reshape(2, 32, GROUP * HD)
    greet(ring_partners(at) + line_partners(at))

    def own(total):
        rows = total.astype(BF16)
        patches[...] = rows
        hidden = rows.astype(F32)
        inv = lax.rsqrt(jnp.mean(hidden * hidden, -1, keepdims=True) + EPS)
        normed[at.t] = (hidden * inv * gain[...].astype(F32)).astype(BF16)

    def patch_chain():
        for i in range(8):
            cols = pl.ds(i * 512, 512)
            part[:, :, cols] = mm(pooled[...], pool_out[:, cols]).astype(BF16).reshape(NX, OWN, 512)
        yield from scatter_x(net, at, part, first, second, own)
        yield from gather_x(net, at, normed)

    wide = [gather_zy(net, at, wq_all), gather_yz(net, at, wq_all)]
    for chain in wide:
        next(chain)
    run([patch_chain(), gather_x(net, at, cots)] + wide)

    for load in loads:
        load.wait()

    def dot_loop(step):
        acc[...] = jnp.zeros_like(acc)

        @pl.loop(0, 8)
        def _(i):
            acc[...] += step(i)

    def columns(i):
        return pl.ds(pl.multiple_of(i * 512, 512), 512)

    def normed_cols(i):
        return normed[:, :, columns(i)].reshape(ROWS, 512)

    dot_loop(lambda i: mm(normed_cols(i), wq_all[i].reshape(512, GROUP * HD)))
    q[...] = acc[...].astype(BF16)
    dot_loop(lambda i: dg(cots[:, :, columns(i)].reshape(ROWS, 512), wo_v[:, columns(i)], NT))
    g[...] = acc[...].astype(BF16)

    acc[...] = jnp.zeros_like(acc)

    @pl.loop(0, 8)
    def _(i):
        rows = normed_cols(i)
        acc[:, 0:HD] += mm(rows, wk_v[columns(i), :])
        acc[:, HD:2 * HD] += mm(rows, wv_v[columns(i), :])

    kv[0] = acc[:, 0:HD].astype(BF16)
    kv[1] = acc[:, HD:2 * HD].astype(BF16)
    net.finish()


def spread_kernel(q, g, kv, kv_all, qb, gb, send, recv):
    at = Place()
    net = Net(send, recv)
    kv_all[at.z, at.y, at.c] = kv[...]
    greet(ring_partners(at) + [{"seq": at.twin}])
    chains = [gather_zy(net, at, kv_all), gather_yz(net, at, kv_all)]
    for chain in chains:
        next(chain)
    swaps = [
        net.put(q.at[pl.ds(HALF, HALF)], qb, seq=at.twin),
        net.put(g.at[pl.ds(HALF, HALF)], gb, seq=at.twin),
    ]
    run(chains)
    for copy in swaps:
        copy.wait_recv()
    net.finish()


def attend_kernel(q, g, qb, gb, kv, oa, ob, dqa, dqb, part, dk, dv):
    s = lax.axis_index("seq")
    rows = GROUP * HALF
    scale = HD ** (-0.5)
    c2 = scale * math.log2(math.e)
    groups = KB // HD
    dk[...] = jnp.zeros_like(dk)
    dv[...] = jnp.zeros_like(dv)

    def stack(ref):
        block = ref[0:HALF, :]
        return jnp.concatenate([block[:, h * HD:(h + 1) * HD] for h in range(GROUP)], 0)

    def unstack(value):
        return jnp.concatenate([value[h * HALF:(h + 1) * HALF] for h in range(GROUP)], 1)

    for q_ref, g_ref, o_ref, dq_ref, base in (
        (q, g, oa, dqa, s * ROWS),
        (qb, gb, ob, dqb, (SHARDS - 1 - s) * ROWS + HALF),
    ):
        qs, gs = stack(q_ref), stack(g_ref)
        qt = qs.T
        gt = gs.T
        pos = base + lax.rem(lax.broadcasted_iota(jnp.int32, (KB, rows), 1), HALF)
        key = lax.broadcasted_iota(jnp.int32, (KB, rows), 0)
        full = lax.div(base, KB)

        def block(j, which):
            return kv[pl.ds(j * groups, groups), which].reshape(KB, HD)

        def scores(j, masked):
            st = mm(block(j, 0), qt) * c2
            if masked:
                st = jnp.where(key + j * KB <= pos, st, NEG)
            return st

        def forward(j, carry, masked):
            top, mass, acc = carry
            st = scores(j, masked)
            new = jnp.maximum(top, jnp.max(st, 0, keepdims=True))
            fade = jnp.exp2(top - new)
            p = jnp.exp2(st - new)
            mass = mass * fade + jnp.sum(p, 0, keepdims=True)
            acc = acc * fade + dg(block(j, 1), p.astype(BF16), TN)
            return new, mass, acc

        carry = (
            jnp.full((1, rows), NEG, F32),
            jnp.zeros((1, rows), F32),
            jnp.zeros((HD, rows), F32),
        )
        carry = lax.fori_loop(0, full, lambda j, c: forward(j, c, False), carry)
        top, mass, acc = forward(full, carry, True)
        lse = top + jnp.log2(mass)
        ot = (acc / mass).astype(BF16)
        o_ref[...] = unstack(ot.T)
        delta = jnp.sum(gt.astype(F32) * ot.astype(F32), 0, keepdims=True)

        def backward(j, dqt, masked):
            prob = jnp.exp2(scores(j, masked) - lse)
            dprob = mm(block(j, 1), gt)
            ds = (prob * (dprob - delta)).astype(BF16)
            at = pl.ds(j * groups, groups)
            dk[at] += mm(ds, qs).reshape(groups, HD, HD)
            dv[at] += mm(prob.astype(BF16), gs).reshape(groups, HD, HD)
            return dqt + dg(block(j, 0), ds, TN)

        dqt = jnp.zeros((HD, rows), F32)
        dqt = lax.fori_loop(0, full, lambda j, c: backward(j, c, False), dqt)
        dqt = backward(full, dqt, True)
        dq_ref[...] = unstack((dqt * scale).T.astype(BF16))

    @pl.loop(0, SHARDS)
    def _(j):
        part[j, 0] = (dk[j] * scale).astype(BF16)
        part[j, 1] = dv[j].astype(BF16)


def collect_kernel(
    part, oa, ob, dqa, dqb, attn, dq, dkv,
    sib, acc0, acc1, ya1, ya2, za1, za2, yb1, yb2, zb1, zb2, send, recv,
):
    at = Place()
    net = Net(send, recv)
    attn[0:HALF, :] = oa[...]
    dq[0:HALF, :] = dqa[...]
    greet(ring_partners(at) + [{"seq": at.twin}])
    near = [
        net.put(part.at[pl.ds(0, NZ), pl.ds(0, NY), 1 - at.c, half], sib.at[half], seq=at.sib)
        for half in (1, 0)
    ]
    swaps = [
        net.put(ob, attn.at[pl.ds(HALF, HALF)], seq=at.twin),
        net.put(dqb, dq.at[pl.ds(HALF, HALF)], seq=at.twin),
    ]
    near[0].wait_recv()

    @pl.loop(0, NZ)
    def _(i):
        acc1[i] = (part[i, :, at.c, 1].astype(F32) + sib[1, i].astype(F32)).astype(BF16)

    later = scatter_zy(net, at, acc1, zb1, zb2, yb1, yb2, dkv.at[1])
    next(later)
    near[1].wait_recv()

    @pl.loop(0, NZ)
    def _(i):
        acc0[:, i] = (part[i, :, at.c, 0].astype(F32) + sib[0, i].astype(F32)).astype(BF16)

    run([scatter_yz(net, at, acc0, ya1, ya2, za1, za2, dkv.at[0]), later])
    for copy in swaps:
        copy.wait_recv()
    net.finish()


def back_kernel(
    attn, dq, dkv, patches, cot, gain, wq, wk, wv, wo,
    layer, grad,
    part, part2, first, second, first2, second2, wq_v, wk_v, wv_v, wo_v, send, recv, local,
):
    at = Place()
    net = Net(send, recv)
    loads = [
        pltpu.make_async_copy(src, dst, local.at[i])
        for i, (src, dst) in enumerate(((wo, wo_v), (wq, wq_v), (wk, wk_v), (wv, wv_v)))
    ]
    for load in loads:
        load.start()
    greet(line_partners(at))
    loads[0].wait()

    @pl.loop(0, 8)
    def _(i):
        cols = pl.ds(pl.multiple_of(i * 512, 512), 512)
        part[:, :, cols] = mm(attn[...], wo_v[:, cols]).astype(BF16).reshape(NX, OWN, 512)

    def layer_result(total):
        layer[...] = (patches[...].astype(F32) + total).astype(BF16)

    def grad_result(total):
        hidden = patches[...].astype(F32)
        inv = lax.rsqrt(jnp.mean(hidden * hidden, -1, keepdims=True) + EPS)
        unit = hidden * inv
        scaled = total * gain[...].astype(F32)
        mean = jnp.mean(scaled * unit, -1, keepdims=True)
        grad[...] = (cot[...].astype(F32) + inv * (scaled - unit * mean)).astype(BF16)

    out_chain = scatter_x(net, at, part, first, second, layer_result)
    next(out_chain)
    for load in loads[1:]:
        load.wait()

    @pl.loop(0, 8)
    def _(i):
        rows = pl.ds(pl.multiple_of(i * 512, 512), 512)
        total = dg(dq[...], wq_v[rows, :], NT)
        total = total + dg(dkv[0], wk_v[rows, :], NT) + dg(dkv[1], wv_v[rows, :], NT)
        part2[:, :, rows] = total.astype(BF16).reshape(NX, OWN, 512)

    run([scatter_x(net, at, part2, first2, second2, grad_result), out_chain])
    net.finish()


def pool_group(byte_block, lengths, pool_query, pool_key, pool_value):
    ends = jnp.cumsum(lengths)
    starts = ends - lengths
    where_at = jnp.arange(byte_block.shape[0], dtype=jnp.int32)
    member = (where_at[None, :] >= starts[:, None]) & (where_at[None, :] < ends[:, None])
    sums = mm(member.astype(BF16), byte_block)
    means = (sums / lengths[:, None].astype(F32)).astype(BF16)
    pool_q = mm(means, pool_query).astype(BF16)
    pool_k = mm(byte_block, pool_key).astype(BF16)
    pool_v = mm(byte_block, pool_value).astype(BF16)
    heads = pool_query.shape[1] // HD
    q_heads = pool_q.reshape(-1, heads, HD)
    k_heads = pool_k.reshape(-1, heads, HD)
    v_heads = pool_v.reshape(-1, heads, HD)
    scores = jnp.einsum("phd,bhd->hpb", q_heads, k_heads, preferred_element_type=F32)
    scores = jnp.where(member[None], scores * HD ** (-0.5), NEG)
    top = jnp.max(scores, -1, keepdims=True)
    expo = jnp.exp(scores - top)
    weights = (expo / jnp.sum(expo, -1, keepdims=True)).astype(BF16)
    pooled = jnp.einsum("hpb,bhd->phd", weights, v_heads, preferred_element_type=F32)
    return pooled.reshape(lengths.shape[0], -1).astype(BF16)


def sds(*shape):
    return jax.ShapeDtypeStruct(shape, BF16)


def buf(*shape):
    return pltpu.VMEM(shape, BF16)


def call(kernel, outs, specs, scratch, collective_id, flops, copies=0, local=0):
    sems = []
    if copies:
        sems = [pltpu.SemaphoreType.DMA((copies,)), pltpu.SemaphoreType.DMA((copies,))]
    if local:
        sems.append(pltpu.SemaphoreType.DMA((local,)))
    here, there = pl.BlockSpec(memory_space=pltpu.VMEM), pl.BlockSpec(memory_space=pl.ANY)
    return pl.pallas_call(
        kernel,
        out_shape=outs,
        in_specs=[here if c == "v" else there for c in specs],
        out_specs=[here] * len(outs),
        scratch_shapes=list(scratch) + sems,
        compiler_params=pltpu.CompilerParams(
            collective_id=collective_id,
            has_side_effects=collective_id is not None,
            vmem_limit_bytes=VMEM,
        ),
        cost_estimate=pl.CostEstimate(flops=flops, bytes_accessed=1 << 23, transcendentals=0),
    )


def front(pooled, pool_out, gain, cot, wq, wk, wv, wo):
    wide = GROUP * HD
    return call(
        front_kernel,
        [sds(ROWS, wide), sds(ROWS, wide), sds(2, ROWS, HD), sds(OWN, D), sds(NZ, NY, 2, 2, 32, wide)],
        "vvvvvaaa",
        [
            buf(NX, OWN, D), buf(NX, OWN, D), buf(NX, OWN, D), buf(2, OWN // 2, D), buf(2, OWN, D),
            pltpu.VMEM((ROWS, wide), F32), buf(D, HD), buf(D, HD), buf(wide, D),
        ],
        1, 2 * 10**9, 64, 3,
    )(pooled, pool_out, gain, cot, wq, wk, wv, wo)


def spread(q, g, kv):
    wide = GROUP * HD
    return call(
        spread_kernel,
        [sds(NZ, NY, 2, 2, ROWS, HD), sds(HALF, wide), sds(HALF, wide)],
        "vvv", [], 2, 10**6, 48,
    )(q, g, kv)


def attend(q, g, qb, gb, kv_all):
    wide = GROUP * HD
    return call(
        attend_kernel,
        [sds(HALF, wide)] * 4 + [sds(SHARDS, 2, ROWS, HD)],
        "vvvvv",
        [pltpu.VMEM((SHARDS, ROWS, HD), F32)] * 2,
        None, 4 * 10**9,
    )(q, g, qb, gb, kv_all)


def collect(part, oa, ob, dqa, dqb):
    wide = GROUP * HD
    half = ROWS // 2
    return call(
        collect_kernel,
        [sds(ROWS, wide), sds(ROWS, wide), sds(2, ROWS, HD)],
        "vvvvv",
        [
            buf(2, NZ, NY, ROWS, HD), buf(NY, NZ, ROWS, HD), buf(NZ, NY, ROWS, HD),
            buf(2, 4, ROWS, HD), buf(2, NZ, ROWS, HD),
            buf(2, half, HD), buf(3, 2, ROWS, HD),
            buf(2, half, HD), buf(2, ROWS, HD),
            buf(2, NY // 2, ROWS, HD), buf(3, 2, NY, ROWS, HD),
        ],
        3, 10**7, 48,
    )(part, oa, ob, dqa, dqb)


def back(attn, dq, dkv, patches, cot, gain, wq, wk, wv, wo):
    wide = GROUP * HD
    return call(
        back_kernel,
        [sds(OWN, D), sds(OWN, D)],
        "vvvvvvaaaa",
        [
            buf(NX, OWN, D), buf(NX, OWN, D), buf(2, OWN // 2, D), buf(2, OWN, D),
            buf(2, OWN // 2, D), buf(2, OWN, D),
            buf(D, wide), buf(D, HD), buf(D, HD), buf(wide, D),
        ],
        4, 2 * 10**9, 16, 4,
    )(attn, dq, dkv, patches, cot, gain, wq, wk, wv, wo)


def on_device(
    byte_rows,
    patch_lengths,
    pool_query,
    pool_key,
    pool_value,
    pool_out,
    norm_gain,
    query_weight,
    key_weight,
    value_weight,
    out_weight,
    cotangent,
):
    pooled = pool_group(byte_rows, patch_lengths[0], pool_query, pool_key, pool_value)
    gain = norm_gain.reshape(1, D)
    q, g, kv, patches, wq_all = front(
        pooled, pool_out, gain, cotangent, query_weight, key_weight, value_weight, out_weight
    )
    kv_all, qb, gb = spread(q, g, kv)
    oa, ob, dqa, dqb, part = attend(q, g, qb, gb, kv_all.reshape(SHARDS, 2, ROWS, HD))
    attn, dq, dkv = collect(part.reshape(NZ, NY, 2, 2, ROWS, HD), oa, ob, dqa, dqb)
    return tuple(
        back(
            attn, dq, dkv, patches, cotangent, gain,
            wq_all.reshape(D, GROUP * HD), key_weight, value_weight, out_weight,
        )
    )


def solution(mesh):
    placed = (
        P("seq", None),
        P("seq", None),
        P(None, "tensor"),
        P(None, "tensor"),
        P(None, "tensor"),
        P("tensor", None),
        P(),
        P("seq", "tensor"),
        P(None, "tensor"),
        P(None, "tensor"),
        P("tensor", None),
        P(("seq", "tensor"), None),
    )
    return jax.shard_map(
        on_device,
        mesh=mesh,
        in_specs=placed,
        out_specs=(P(("seq", "tensor"), None), P(("seq", "tensor"), None)),
        check_vma=False,
    )
```

time: 759 us -> 197 us (0.26)
  waiting for transfers between devices: 315 us -> 0 us
  Pallas kernels: 0 us -> 183 us
  matrix products: 183 us -> 4.83 us
  blocking collectives: 104 us -> 0 us
  local copies, waits for them, and re-layouts: 99.3 us -> 6.16 us
  other arithmetic: 29.6 us -> 1.84 us
  between operations: 14.5 us -> 0.74 us
    all_gather x7 -> x0, waiting for transfers between devices: 235 us -> none  [the longest x1 75.2 us: on_device(): query_full = lax.all_gather(query_weight, 'seq', axis=0, tiled=True)]
    pallas_call x0 -> x5, Pallas kernels: none -> 183 us  [the longest x1 54.4 us: front(): call(front_kernel, [sds(ROWS, wide), sds(ROWS, wide), sds(2, ROWS, HD), s...]
    dot_general x70 -> x5, matrix products: 183 us -> 4.43 us  [the longest x3 3.59 us: mm(): return jnp.dot(a, b, preferred_element_type=F32)]
    all_gather x2 -> x0, blocking collectives: 104 us -> none  [the longest x1 52.3 us: on_device(): lax.all_gather(delta, 'seq', axis=1, tiled=True)]
    reduce_scatter x3 -> x0, waiting for transfers between devices: 78.8 us -> none  [the longest x1 33.4 us: on_device(): lax.psum_scatter(partial_value, 'tensor', scatter_dimension=0, tiled=True)]
    dynamic_slice x40 -> x0, local copies, waits for them, and re-layouts: 66.4 us -> none  [the longest x16 39.2 us: step(): g_rows = lax.dynamic_slice_in_dim(g_piece, at, sub, 0)]
    reshape x17 -> x1, local copies, waits for them, and re-layouts: 27.4 us -> 1.31 us  [on_device(): gain = norm_gain.reshape(1, D)]
    reduce_sum x11 -> x0, other arithmetic: 18.9 us -> none  [the longest x8 16.4 us: max_pass(): jnp.sum(jnp.exp(scores - new_top[..., None]), -1)]
  transfers between devices with their start and end apart: 10 -> 0, of which waited for: 8 -> 0; matrix products, arithmetic and copies ran while one was open for 17% -> 0% of each run, Pallas kernels for 0% -> 0%
where the time goes in v1:
time: 197 us; the launch traced here: 196 us
  Pallas kernels  183 us (93%)
  local copies, waits for them, and re-layouts  6.16 us (3%)
  matrix products  4.83 us (2%)
    pallas_call x1, Pallas kernels, front(): call(front_kernel, [sds(ROWS, wide), sds(ROWS, wide), sds(2, ROWS, HD), s...  54.4 us
    pallas_call x1, Pallas kernels, collect(): call(collect_kernel, [sds(ROWS, wide), sds(ROWS, wide), sds(2, ROWS, HD)]...  39.6 us
    pallas_call x1, Pallas kernels, spread(): call(spread_kernel, [sds(NZ, NY, 2, 2, ROWS, HD), sds(HALF, wide), sds(HA...  39 us
    pallas_call x1, Pallas kernels, back(): call(back_kernel, [sds(OWN, D), sds(OWN, D)], 'vvvvvvaaaa', [buf(NX, OWN,...  26.6 us
    pallas_call x1, Pallas kernels, attend(): call(attend_kernel, [sds(HALF, wide)] * 4 + [sds(SHARDS, 2, ROWS, HD)], '...  23 us

profile of v1, /device:TPU:2, one launch (start us, length us, event | category | flops | bytes accessed | tf_op | source)
XLA Modules:
  0.0 196.3 jit_solution(6117141777765449494)
XLA Ops:
  0.6 0.0 copy-start
  0.6 0.0 copy-start.1
  0.7 0.8 bitcast_convert_fusion
  1.4 1.3 reshape.109.gain
  2.7 0.8 copy.18
  3.5 0.2 reduce-window.7
  3.7 0.1 reduce
  3.8 0.7 bitcast_subtract_fusion
  4.4 0.0 copy-done
  4.4 1.6 fusion.7
  6.0 0.1 fusion.9
  6.2 1.5 convolution_convert_fusion
  7.7 0.4 fusion.19
  8.1 0.2 fusion.3
  8.3 0.5 convolution_convert_fusion.1
  8.8 0.6 convolution_convert_fusion.2
  9.5 0.7 copy.23.pooled
  10.2 54.4 %shard_map.131 = (bf16[128,512]{1,0:T(8,128)(2,1)}, bf16[128,512]{1,0:T(8,128)(2,1)}, bf16[2,128,128]{2,1,0:T(8,128)(2,1)}, bf16[32,4096]{1,0:T(8,128)(2,1)}, bf16[8,4,2,2,32,512]{5,4,3,2,1,0:T(8,128)(2,1)}) custom-call(bf16[128,256]{1,0:T(8,128)(2,1)} %copy.23.pooled, bf16[256,4096]{1,0:T(8,128)(2,1)} %pool_out.1, bf16[1,4096]{1,0:T(2,128)(2,1)} %reshape.109.gain, ...), custom_call_target="tpu_custom_call" | custom-call | flops 2000000000 | bytes 8388608 | tf_op jit(solution)/shard_map/pallas_call | solution.py:599
  64.6 39.0 %shard_map.132 = (bf16[8,4,2,2,128,128]{5,4,3,2,1,0:T(8,128)(2,1)}, bf16[64,512]{1,0:T(8,128)(2,1)}, bf16[64,512]{1,0:T(8,128)(2,1)}) custom-call(bf16[128,512]{1,0:T(8,128)(2,1)} %get-tuple-element.18.q, bf16[128,512]{1,0:T(8,128)(2,1)} %get-tuple-element.19.g, bf16[2,128,128]{2,1,0:T(8,128)(2,1)} %get-tuple-element.20.kv), custom_call_target="tpu_custom_call" | custom-call | flops 1000000 | bytes 8388608 | tf_op jit(solution)/shard_map/pallas_call | solution.py:613
  103.7 23.0 %shard_map.133 = (bf16[64,512]{1,0:T(8,128)(2,1)}, bf16[64,512]{1,0:T(8,128)(2,1)}, bf16[64,512]{1,0:T(8,128)(2,1)}, bf16[64,512]{1,0:T(8,128)(2,1)}, bf16[64,2,128,128]{3,2,1,0:T(8,128)(2,1)}) custom-call(bf16[128,512]{1,0:T(8,128)(2,1)} %get-tuple-element.18.q, bf16[128,512]{1,0:T(8,128)(2,1)} %get-tuple-element.19.g, ...), custom_call_target="tpu_custom_call" | custom-call | flops 4000000000 | bytes 8388608 | tf_op jit(solution)/shard_map/pallas_call | solution.py:622
  126.7 39.6 %shard_map.134 = (bf16[128,512]{1,0:T(8,128)(2,1)}, bf16[128,512]{1,0:T(8,128)(2,1)}, bf16[2,128,128]{2,1,0:T(8,128)(2,1)}) custom-call(bf16[8,4,2,2,128,128]{5,4,3,2,1,0:T(8,128)(2,1)} %bitcast.32, bf16[64,512]{1,0:T(8,128)(2,1)} %get-tuple-element.25.oa, bf16[64,512]{1,0:T(8,128)(2,1)} %get-tuple-element.26.ob, bf16[64,512]{1,0:T(8,128)(2,1)} %get-tuple-element.27.dqa, ...), custom_call_target="tpu_custom_call" | custom-call | flops 10000000 | bytes 8388608 | tf_op jit(solution)/shard_map/pallas_call | solution.py:634
  166.3 26.6 %shard_map.135 = (bf16[32,4096]{1,0:T(8,128)(2,1)}, bf16[32,4096]{1,0:T(8,128)(2,1)}) custom-call(bf16[128,512]{1,0:T(8,128)(2,1)} %get-tuple-element.29.attn, bf16[128,512]{1,0:T(8,128)(2,1)} %get-tuple-element.30.dq, bf16[2,128,128]{2,1,0:T(8,128)(2,1)} %get-tuple-element.31.dkv, bf16[32,4096]{1,0:T(8,128)(2,1)} %get-tuple-element.32.patches, ...), custom_call_target="tpu_custom_call" | custom-call | flops 2000000000 | bytes 8388608 | tf_op jit(solution)/shard_map/pallas_call | solution.py:651
  193.0 1.7 copy.35
  194.6 1.7 copy.36
  (1 shorter events, 0.0 us)
Async XLA Ops:
  0.6 3.8 %copy-start = (bf16[512,1024]{1,0:T(8,128)(2,1)S(1)}, bf16[512,1024]{1,0:T(8,128)(2,1)}, u32[]{:S(2)}) copy-start(bf16[512,1024]{1,0:T(8,128)(2,1)} %param.12) | copy-start | bytes 3145732
  0.6 7.7 %copy-start.1 = (bf16[1024,256]{1,0:T(8,128)(2,1)S(1)}, bf16[1024,256]{1,0:T(8,128)(2,1)}, u32[]{:S(2)}) copy-start(bf16[1024,256]{1,0:T(8,128)(2,1)} %param.16) | copy-start | bytes 1572868

commit v2 on v0

v2 whole, which is shorter than its diff:
```python
import math

import jax
import jax.numpy as jnp
from jax import lax
from jax.experimental import pallas as pl
from jax.experimental.pallas import tpu as pltpu
from jax.sharding import PartitionSpec as P

EPS = 1e-05
NEG = -1e30
MESH = pl.DeviceIdType.MESH
NZ, NY, NX = 8, 4, 4
HD = 128
GROUP = 4
ROWS = 128
HALF = 64
SHARDS = 64
D = 4096
OWN = 32
KB = 512
VMEM = 56 * 1024 * 1024
F32 = jnp.float32
BF16 = jnp.bfloat16
NT = (((1,), (1,)), ((), ()))
TN = (((0,), (0,)), ((), ()))


def mm(a, b):
    return jnp.dot(a, b, preferred_element_type=F32)


def dg(a, b, dims):
    return lax.dot_general(a, b, dims, preferred_element_type=F32)


class Place:
    def __init__(self):
        s = lax.axis_index("seq")
        self.s = s
        self.z = lax.div(s, 8)
        self.y = lax.rem(lax.div(s, 2), 4)
        self.c = lax.rem(s, 2)
        self.t = lax.axis_index("tensor")
        self.sib = self.seq(self.z, self.y, 1 - self.c)
        self.up = self.seq(self.zz(1), self.y, self.c)
        self.down = self.seq(self.zz(-1), self.y, self.c)
        self.north = self.seq(self.z, self.yy(1), self.c)
        self.south = self.seq(self.z, self.yy(-1), self.c)
        self.twin = SHARDS - 1 - s

    def zz(self, i):
        return lax.rem(self.z + NZ + i, NZ)

    def yy(self, i):
        return lax.rem(self.y + NY + i, NY)

    def tt(self, i):
        return lax.rem(self.t + NX + i, NX)

    def seq(self, z, y, c):
        return (z * NY + y) * 2 + c


class Net:
    def __init__(self, send, recv):
        self.send, self.recv, self.all = send, recv, []

    def put(self, src, dst, **device):
        n = len(self.all)
        copy = pltpu.make_async_remote_copy(
            src_ref=src,
            dst_ref=dst,
            send_sem=self.send.at[n],
            recv_sem=self.recv.at[n],
            device_id=device,
            device_id_type=MESH,
        )
        copy.start()
        self.all.append(copy)
        return copy

    def finish(self):
        for copy in self.all:
            copy.wait_send()


def greet(devices):
    barrier = pltpu.get_barrier_semaphore()
    for device in devices:
        pl.semaphore_signal(barrier, inc=1, device_id=device, device_id_type=MESH)
    pl.semaphore_wait(barrier, len(devices))


def partners(at):
    ring = [{"seq": d} for d in (at.sib, at.up, at.down, at.north, at.south, at.twin)]
    return ring + [{"tensor": at.tt(1)}, {"tensor": at.tt(-1)}]


def run(chains):
    chains = list(chains)
    while chains:
        left = []
        for chain in chains:
            try:
                next(chain)
                left.append(chain)
            except StopIteration:
                pass
        chains = left


def same(net, view, **device):
    return net.put(view, view, **device)


def gather_zy(net, at, buf):
    rows = buf.shape[4] // 2
    zz, yy, c, y = at.zz, at.yy, at.c, at.y
    for i in range(1, 4):
        p = same(net, buf.at[0, zz(1 - i), y, c], seq=at.up)
        m = same(net, buf.at[0, zz(i - 1), y, c], seq=at.down)
        yield
        p.wait_recv()
        m.wait_recv()
    p = same(net, buf.at[0, zz(-3), y, c, pl.ds(0, rows)], seq=at.up)
    m = same(net, buf.at[0, zz(3), y, c, pl.ds(rows, rows)], seq=at.down)
    yield
    p.wait_recv()
    m.wait_recv()
    every = pl.ds(0, NZ)
    p = same(net, buf.at[0, every, y, c], seq=at.north)
    m = same(net, buf.at[0, every, y, c], seq=at.south)
    sib = [same(net, buf.at[0, every, y, c], seq=at.sib)]
    yield
    p.wait_recv()
    m.wait_recv()
    p = same(net, buf.at[0, pl.ds(0, 4), yy(-1), c], seq=at.north)
    m = same(net, buf.at[0, pl.ds(4, 4), yy(1), c], seq=at.south)
    sib.append(same(net, buf.at[0, every, yy(-1), c], seq=at.sib))
    sib.append(same(net, buf.at[0, every, yy(1), c], seq=at.sib))
    yield
    p.wait_recv()
    m.wait_recv()
    sib.append(same(net, buf.at[0, every, yy(2), c], seq=at.sib))
    yield
    for copy in sib:
        copy.wait_recv()


def gather_yz(net, at, buf):
    rows = buf.shape[4] // 2
    zz, yy, c, z = at.zz, at.yy, at.c, at.z
    p = same(net, buf.at[1, z, at.y, c], seq=at.north)
    m = same(net, buf.at[1, z, at.y, c], seq=at.south)
    yield ()
    p.wait_recv()
    m.wait_recv()
    p = same(net, buf.at[1, z, yy(-1), c, pl.ds(0, rows)], seq=at.north)
    m = same(net, buf.at[1, z, yy(1), c, pl.ds(rows, rows)], seq=at.south)
    yield ()
    p.wait_recv()
    m.wait_recv()
    every = pl.ds(0, NY)
    sib, offsets = [same(net, buf.at[1, z, every, c], seq=at.sib)], (0,)
    for i in range(1, 5):
        if i < 4:
            p = same(net, buf.at[1, zz(1 - i), every, c], seq=at.up)
            m = same(net, buf.at[1, zz(i - 1), every, c], seq=at.down)
        else:
            p = same(net, buf.at[1, zz(-3), pl.ds(0, 2), c], seq=at.up)
            m = same(net, buf.at[1, zz(3), pl.ds(2, 2), c], seq=at.down)
        for copy in sib:
            copy.wait_recv()
        yield offsets
        p.wait_recv()
        m.wait_recv()
        offsets = (i, -i) if i < 4 else (4,)
        sib = [same(net, buf.at[1, zz(o), every, c], seq=at.sib) for o in offsets]
    yield ()
    for copy in sib:
        copy.wait_recv()
    yield offsets


def gather_x(net, at, buf, row):
    tt = at.tt
    rows, low, high = pl.ds(row, 16), pl.ds(0, D // 2), pl.ds(D // 2, D // 2)
    p = same(net, buf.at[at.t, rows], tensor=tt(1))
    m = same(net, buf.at[at.t, rows], tensor=tt(-1))
    yield
    p.wait_recv()
    m.wait_recv()
    p = same(net, buf.at[tt(-1), rows, low], tensor=tt(1))
    m = same(net, buf.at[tt(1), rows, high], tensor=tt(-1))
    yield
    p.wait_recv()
    m.wait_recv()


def add_into(ref, *others):
    total = ref[...].astype(F32)
    for other in others:
        total = total + other[...].astype(F32)
    ref[...] = total.astype(BF16)


def scatter_x(net, at, part, row, first, second, result):
    tt = at.tt
    rows, low, high = pl.ds(row, 16), pl.ds(0, D // 2), pl.ds(D // 2, D // 2)
    p = net.put(part.at[tt(2), rows, low], first.at[0], tensor=tt(1))
    m = net.put(part.at[tt(2), rows, high], first.at[1], tensor=tt(-1))
    yield
    p.wait_recv()
    add_into(part.at[tt(1), rows, low], first.at[0])
    p = net.put(part.at[tt(1), rows], second.at[0], tensor=tt(1))
    m.wait_recv()
    add_into(part.at[tt(-1), rows, high], first.at[1])
    m = net.put(part.at[tt(-1), rows], second.at[1], tensor=tt(-1))
    yield
    p.wait_recv()
    m.wait_recv()
    mine = part[at.t, rows, :].astype(F32)
    result(row, mine + second[0].astype(F32) + second[1].astype(F32))


def scatter_yz(net, at, part, sib, acc, y_first, y_second, z_first, z_next, out):
    yy, zz = at.yy, at.zz
    low, high = pl.ds(0, 4), pl.ds(4, 4)
    order = (yy(2), yy(1), yy(-1), yy(0))
    near = [
        net.put(part.at[0, pl.ds(0, NZ), y, 1 - at.c], sib.at[y], seq=at.sib) for y in order
    ]
    yield

    def own(k):
        near[k].wait_recv()
        y = order[k]
        acc[y] = (part[0, :, y, at.c].astype(F32) + sib[y].astype(F32)).astype(BF16)

    own(0)
    p = net.put(acc.at[yy(2), low], y_first.at[0], seq=at.north)
    m = net.put(acc.at[yy(2), high], y_first.at[1], seq=at.south)
    own(1)
    own(2)
    yield
    p.wait_recv()
    add_into(acc.at[yy(1), low], y_first.at[0])
    p = net.put(acc.at[yy(1)], y_second.at[0], seq=at.north)
    m.wait_recv()
    add_into(acc.at[yy(-1), high], y_first.at[1])
    m = net.put(acc.at[yy(-1)], y_second.at[1], seq=at.south)
    own(3)
    yield
    p.wait_recv()
    m.wait_recv()
    add_into(acc.at[at.y], y_second.at[0], y_second.at[1])
    mine = acc.at[at.y]
    low, high = pl.ds(0, 1), pl.ds(1, 1)
    p = net.put(mine.at[zz(4), low], z_first.at[0], seq=at.up)
    m = net.put(mine.at[zz(4), high], z_first.at[1], seq=at.down)
    yield
    p.wait_recv()
    m.wait_recv()
    add_into(mine.at[zz(3), low], z_first.at[0])
    add_into(mine.at[zz(-3), high], z_first.at[1])
    for i in (3, 2, 1):
        p = net.put(mine.at[zz(i)], z_next.at[i - 1, 0], seq=at.up)
        m = net.put(mine.at[zz(-i)], z_next.at[i - 1, 1], seq=at.down)
        yield
        p.wait_recv()
        m.wait_recv()
        if i > 1:
            add_into(mine.at[zz(i - 1)], z_next.at[i - 1, 0])
            add_into(mine.at[zz(1 - i)], z_next.at[i - 1, 1])
    total = mine[at.z].astype(F32) + z_next[0, 0].astype(F32) + z_next[0, 1].astype(F32)
    out(0, total)


def scatter_zy(net, at, part, sib, acc, z_first, z_next, y_first, y_second, out):
    zz, yy = at.zz, at.yy
    every = pl.ds(0, NY)
    low, high = pl.ds(0, 2), pl.ds(2, 2)

    def share(*offsets):
        return [
            (o, net.put(part.at[1, zz(o), every, 1 - at.c], sib.at[zz(o)], seq=at.sib)) for o in offsets
        ]

    def own(near):
        for o, copy in near:
            copy.wait_recv()
            z = zz(o)
            acc[z] = (part[1, z, :, at.c].astype(F32) + sib[z].astype(F32)).astype(BF16)

    yield (4,)
    near = share(4)
    yield (3, -3)
    own(near)
    near = share(3, -3)
    p = net.put(acc.at[zz(4), low], z_first.at[0], seq=at.up)
    m = net.put(acc.at[zz(4), high], z_first.at[1], seq=at.down)
    for i in (3, 2, 1):
        yield (i - 1, 1 - i) if i > 1 else (0,)
        own(near)
        near = share(i - 1, 1 - i) if i > 1 else share(0)
        p.wait_recv()
        m.wait_recv()
        if i == 3:
            add_into(acc.at[zz(3), low], z_first.at[0])
            add_into(acc.at[zz(-3), high], z_first.at[1])
        else:
            add_into(acc.at[zz(i)], z_next.at[i, 0])
            add_into(acc.at[zz(-i)], z_next.at[i, 1])
        p = net.put(acc.at[zz(i)], z_next.at[i - 1, 0], seq=at.up)
        m = net.put(acc.at[zz(-i)], z_next.at[i - 1, 1], seq=at.down)
    yield ()
    own(near)
    p.wait_recv()
    m.wait_recv()
    mine = acc.at[at.z]
    add_into(mine, z_next.at[0, 0], z_next.at[0, 1])
    p = net.put(mine.at[yy(2), pl.ds(0, 1)], y_first.at[0], seq=at.north)
    m = net.put(mine.at[yy(2), pl.ds(1, 1)], y_first.at[1], seq=at.south)
    yield ()
    p.wait_recv()
    m.wait_recv()
    add_into(mine.at[yy(1), pl.ds(0, 1)], y_first.at[0])
    add_into(mine.at[yy(-1), pl.ds(1, 1)], y_first.at[1])
    p = net.put(mine.at[yy(1)], y_second.at[0], seq=at.north)
    m = net.put(mine.at[yy(-1)], y_second.at[1], seq=at.south)
    yield ()
    p.wait_recv()
    m.wait_recv()
    out(1, mine[at.y].astype(F32) + y_second[0].astype(F32) + y_second[1].astype(F32))


def pool(lengths, byte, pool_query, pool_key, pool_value):
    nb = byte.shape[0]
    count = lengths[...].astype(F32)
    row = lax.broadcasted_iota(jnp.int32, (ROWS, ROWS), 0)
    col = lax.broadcasted_iota(jnp.int32, (ROWS, ROWS), 1)
    ends = jnp.sum(jnp.where(col <= row, count, 0.0), 1, keepdims=True)
    size = jnp.sum(jnp.where(col == row, count, 0.0), 1, keepdims=True)
    where_at = lax.broadcasted_iota(jnp.int32, (ROWS, nb), 1).astype(F32)
    member = (where_at >= ends - size) & (where_at < ends)
    sums = mm(jnp.where(member, 1.0, 0.0).astype(BF16), byte[...])
    means = (sums / size).astype(BF16)
    pq = mm(means, pool_query[...]).astype(BF16)
    pk = mm(byte[...], pool_key[...]).astype(BF16)
    pv = mm(byte[...], pool_value[...]).astype(BF16)
    heads = []
    for h in range(pq.shape[1] // HD):
        cols = slice(h * HD, (h + 1) * HD)
        scores = jnp.where(member, dg(pq[:, cols], pk[:, cols], NT) * HD ** (-0.5), NEG)
        expo = jnp.exp(scores - jnp.max(scores, -1, keepdims=True))
        weights = (expo / jnp.sum(expo, -1, keepdims=True)).astype(BF16)
        heads.append(mm(weights, pv[:, cols]))
    return jnp.concatenate(heads, 1).astype(BF16)


def stack(block):
    return jnp.concatenate([block[:, h * HD:(h + 1) * HD] for h in range(GROUP)], 0)


def unstack(value):
    return jnp.concatenate([value[h * HALF:(h + 1) * HALF] for h in range(GROUP)], 1)


def columns(i):
    return pl.ds(pl.multiple_of(i * 512, 512), 512)


def kernel(
    lengths, gain, byte_h, pq_h, pk_h, pv_h, po_h, wq_h, wk_h, wv_h, wo_h, cot_h,
    layer, grad,
    byte, pool_q, pool_k, pool_v, pool_o, wk, wv, wo, pooled, patches, normed, cots, wq,
    part, first, second, part2, first2, second2, part3, first3, second3, grad_acc,
    acc, q, g, qb, gb, attn, dq, ob, dqb,
    kvb, qs, qt, gs, gt, top, mass, oacc, lse, delta, dqt, dkv_acc, ahead,
    pgrad, sib0, sib1, acc0, acc1, ya1, ya2, za1, za2, yb1, yb2, zb1, zb2, dkv,
    send, recv, local,
):
    at = Place()
    net = Net(send, recv)
    c2 = HD ** (-0.5) * math.log2(math.e)
    loads = {}

    def load(name, src, dst):
        copy = pltpu.make_async_copy(src, dst, local.at[len(loads)])
        copy.start()
        loads[name] = copy

    def ready(*names):
        for name in names:
            loads[name].wait()

    for half in range(2):
        load("wq%d" % half, wq_h.at[pl.ds(half * 32, 32)], wq.at[half, at.z, at.y, at.c])
    load("byte", byte_h, byte)
    load("pq", pq_h, pool_q)
    load("pk", pk_h, pool_k)
    load("pv", pv_h, pool_v)
    load("po", po_h, pool_o)
    load("cot", cot_h, cots.at[at.t])
    load("wk", wk_h, wk)
    load("wv", wv_h, wv)
    load("wo", wo_h, wo)
    greet(partners(at))

    ready("wq0", "wq1")
    w0, w1 = gather_zy(net, at, wq), gather_yz(net, at, wq)
    next(w0)
    next(w1)

    ready("byte", "pq", "pk", "pv")
    pooled[...] = pool(lengths, byte, pool_q, pool_k, pool_v)
    next(w0)
    next(w1)
    ready("po")
    for i in range(8):
        cols = pl.ds(i * 512, 512)
        part[:, :, cols] = mm(pooled[...], pool_o[:, cols]).astype(BF16).reshape(NX, OWN, 512)

    def own(row, total):
        rows = total.astype(BF16)
        patches[pl.ds(row, 16), :] = rows
        hidden = rows.astype(F32)
        inv = lax.rsqrt(jnp.mean(hidden * hidden, -1, keepdims=True) + EPS)
        normed[at.t, pl.ds(row, 16), :] = (hidden * inv * gain[...].astype(F32)).astype(BF16)

    def patch_chain(k):
        yield from scatter_x(net, at, part, 16 * k, first.at[k], second.at[k], own)
        yield from gather_x(net, at, normed, 16 * k)

    run([patch_chain(0), patch_chain(1), w0, w1])

    def normed_cols(i):
        return normed[:, :, columns(i)].reshape(ROWS, 512)

    ready("wk", "wv", "cot", "wo")
    acc[...] = jnp.zeros_like(acc)

    @pl.loop(0, 8)
    def _(i):
        rows = normed_cols(i)
        acc[:, 0:HD] += mm(rows, wk[columns(i), :])
        acc[:, HD:2 * HD] += mm(rows, wv[columns(i), :])

    for half in range(2):
        for which in range(2):
            block = acc[half * HALF:(half + 1) * HALF, which * HD:(which + 1) * HD]
            kvb[half, at.z, at.y, at.c, which] = block.astype(BF16)
    k0, k1 = gather_zy(net, at, kvb), gather_yz(net, at, kvb)
    next(k1)
    next(k0)
    cot_chains = [gather_x(net, at, cots, 0), gather_x(net, at, cots, 16)]
    for chain in cot_chains:
        next(chain)

    acc[...] = jnp.zeros_like(acc)

    @pl.loop(0, 8)
    def _(i):
        w = jnp.concatenate([wq[half, i, y, c] for y in range(NY) for c in range(2) for half in range(2)], 0)
        acc[...] += mm(normed_cols(i), w)

    q[...] = acc[...].astype(BF16)
    q_swap = net.put(q.at[pl.ds(HALF, HALF)], qb, seq=at.twin)
    next(k1)
    next(k0)

    def prepare(st, block, straight, turned):
        straight[st] = stack(block)
        turned[st] = straight[st].T

    prepare(0, q[0:HALF, :], qs, qt)
    top[...] = jnp.full_like(top, NEG)
    mass[...] = jnp.zeros_like(mass)
    oacc[...] = jnp.zeros_like(oacc)
    for chain in cot_chains:
        next(chain)
    offsets = next(k1)
    next(k0)
    q_swap.wait_recv()
    prepare(1, qb[...], qs, qt)

    column = lax.broadcasted_iota(jnp.int32, (KB, GROUP * HALF), 1)
    key = lax.broadcasted_iota(jnp.int32, (KB, GROUP * HALF), 0)
    ahead[...] = (key >> 6) * ROWS + (key & (HALF - 1)) - (column & (HALF - 1))

    def keys(half, z, which):
        return kvb[half, z, :, :, which].reshape(KB, HD)

    def scores(half, z, st, masked):
        out = mm(keys(half, z, 0), qt[st]) * c2
        if masked:
            mine, other = lax.rem(at.s, 8) * ROWS, lax.rem(at.twin, 8) * ROWS + HALF
            base = mine + st * (other - mine) - half * HALF
            out = jnp.where(ahead[...] <= base, out, NEG)
        return out

    def forward(half, z, st, masked):
        out = scores(half, z, st, masked)
        old = top[st]
        new = jnp.maximum(old, jnp.max(out, 0, keepdims=True))
        fade = jnp.exp2(old - new)
        p = jnp.exp2(out - new)
        mass[st] = mass[st] * fade + jnp.sum(p, 0, keepdims=True)
        oacc[st] = oacc[st] * fade + dg(keys(half, z, 1), p.astype(BF16), TN)
        top[st] = new

    def backward(half, z, st, masked):
        prob = jnp.exp2(scores(half, z, st, masked) - lse[st])
        dprob = mm(keys(half, z, 1), gt[st])
        ds = (prob * (dprob - delta[st])).astype(BF16)
        dkv_acc[0] += mm(ds, qs[st])
        dkv_acc[1] += mm(prob.astype(BF16), gs[st])
        dqt[st] += dg(keys(half, z, 0), ds, TN)

    def tasks(body, half, z):
        @pl.loop(0, 2)
        def _(st):
            last = at.z + st * (NZ - 1 - 2 * at.z)

            @pl.when(z < last)
            def _():
                body(half, z, st, False)

            @pl.when(z == last)
            def _():
                body(half, z, st, True)

    def groups(body, offsets):
        if len(offsets) == 1:
            body(at.zz(offsets[0]))
        elif offsets:

            @pl.loop(0, 2)
            def _(k):
                body(at.zz(offsets[0] * (1 - 2 * k)))

    def forward_group(half, z):
        tasks(forward, half, z)

    steps = 0
    while offsets is not None:
        groups(lambda z: forward_group(1, z), offsets)
        if k0 is not None:
            try:
                next(k0)
            except StopIteration:
                k0 = None

                @pl.loop(0, NZ)
                def _(z):
                    forward_group(0, z)
        if steps == 0:
            for chain in cot_chains:
                next(chain, None)
            acc[...] = jnp.zeros_like(acc)

            @pl.loop(0, 8)
            def _(i):
                acc[...] += dg(cots[:, :, columns(i)].reshape(ROWS, 512), wo[:, columns(i)], NT)

            g[...] = acc[...].astype(BF16)
            g_swap = net.put(g.at[pl.ds(HALF, HALF)], gb, seq=at.twin)
        steps += 1
        offsets = next(k1, None)
    assert k0 is None

    prepare(0, g[0:HALF, :], gs, gt)
    g_swap.wait_recv()
    prepare(1, gb[...], gs, gt)
    for st in range(2):
        ot = (oacc[st] / mass[st]).astype(BF16)
        lse[st] = top[st] + jnp.log2(mass[st])
        delta[st] = jnp.sum(gt[st].astype(F32) * ot.astype(F32), 0, keepdims=True)
        if st == 0:
            attn[0:HALF, :] = unstack(ot.T)
        else:
            ob[...] = unstack(ot.T)
    o_swap = net.put(ob, attn.at[pl.ds(HALF, HALF)], seq=at.twin)
    dqt[...] = jnp.zeros_like(dqt)

    def backward_group(half, z):
        dkv_acc[...] = jnp.zeros_like(dkv_acc)
        tasks(backward, half, z)
        pgrad[half, z, :, :, 0] = (dkv_acc[0] * HD ** (-0.5)).astype(BF16).reshape(NY, 2, HALF, HD)
        pgrad[half, z, :, :, 1] = dkv_acc[1].astype(BF16).reshape(NY, 2, HALF, HD)

    @pl.loop(0, NZ)
    def _(z):
        backward_group(0, z)

    def out(half, total):
        dkv[0, pl.ds(half * HALF, HALF), :] = total[0].astype(BF16)
        dkv[1, pl.ds(half * HALF, HALF), :] = total[1].astype(BF16)

    r0 = scatter_yz(net, at, pgrad, sib0, acc0, ya1, ya2, za1, za2, out)
    next(r0)
    o_swap.wait_recv()

    @pl.loop(0, 8)
    def _(i):
        cols = columns(i)
        part2[:, :, cols] = mm(attn[...], wo[:, cols]).astype(BF16).reshape(NX, OWN, 512)

    def layer_result(row, total):
        rows = pl.ds(row, 16)
        layer[rows, :] = (patches[rows, :].astype(F32) + total).astype(BF16)

    lay = [scatter_x(net, at, part2, 16 * k, first2.at[k], second2.at[k], layer_result) for k in range(2)]
    for chain in lay:
        next(chain)
    r1 = scatter_zy(net, at, pgrad, sib1, acc1, zb1, zb2, yb1, yb2, out)
    computed = 0
    while computed < NZ:
        offsets = next(r1)
        groups(lambda z: backward_group(1, z), offsets)
        computed += len(offsets)
        next(r0, None)
        for chain in lay:
            next(chain, None)

    attn_dq = (dqt[0] * HD ** (-0.5)).T.astype(BF16)
    dq[0:HALF, :] = unstack(attn_dq)
    dqb[...] = unstack((dqt[1] * HD ** (-0.5)).T.astype(BF16))
    dq_swap = net.put(dqb, dq.at[pl.ds(HALF, HALF)], seq=at.twin)
    next(r1)
    next(r0, None)
    dq_swap.wait_recv()

    @pl.loop(0, 8)
    def _(i):
        w = jnp.concatenate([wq[half, i, y, c] for y in range(NY) for c in range(2) for half in range(2)], 0)
        grad_acc[:, columns(i)] = dg(dq[...], w, NT)

    run([r1, r0] + lay)

    @pl.loop(0, 8)
    def _(i):
        rows = columns(i)
        total = grad_acc[:, rows] + dg(dkv[0], wk[rows, :], NT) + dg(dkv[1], wv[rows, :], NT)
        part3[:, :, rows] = total.astype(BF16).reshape(NX, OWN, 512)

    def grad_result(row, total):
        rows = pl.ds(row, 16)
        hidden = patches[rows, :].astype(F32)
        inv = lax.rsqrt(jnp.mean(hidden * hidden, -1, keepdims=True) + EPS)
        unit = hidden * inv
        scaled = total * gain[...].astype(F32)
        mean = jnp.mean(scaled * unit, -1, keepdims=True)
        cot = cots[at.t, rows, :].astype(F32)
        grad[rows, :] = (cot + inv * (scaled - unit * mean)).astype(BF16)

    run([scatter_x(net, at, part3, 16 * k, first3.at[k], second3.at[k], grad_result) for k in range(2)])
    net.finish()


def buf(*shape):
    return pltpu.VMEM(shape, BF16)


def wide(*shape):
    return pltpu.VMEM(shape, F32)


def on_device(
    byte_rows,
    patch_lengths,
    pool_query,
    pool_key,
    pool_value,
    pool_out,
    norm_gain,
    query_weight,
    key_weight,
    value_weight,
    out_weight,
    cotangent,
):
    heads = GROUP * HD
    here, there = pl.BlockSpec(memory_space=pltpu.VMEM), pl.BlockSpec(memory_space=pl.ANY)
    line = [buf(NX, OWN, D), buf(2, 2, 16, D // 2), buf(2, 2, 16, D)]
    half = (2, HALF, HD)
    scratch = [
        buf(*byte_rows.shape), buf(*pool_query.shape), buf(*pool_key.shape), buf(*pool_value.shape),
        buf(*pool_out.shape), buf(*key_weight.shape), buf(*value_weight.shape), buf(*out_weight.shape),
        buf(ROWS, 2 * HD), buf(OWN, D), buf(NX, OWN, D), buf(NX, OWN, D), buf(2, NZ, NY, 2, 32, heads),
        *line, *line, *line, wide(ROWS, D),
        wide(ROWS, heads), buf(ROWS, heads), buf(ROWS, heads), buf(HALF, heads), buf(HALF, heads),
        buf(ROWS, heads), buf(ROWS, heads), buf(HALF, heads), buf(HALF, heads),
        buf(2, NZ, NY, 2, *half), buf(2, GROUP * HALF, HD), buf(2, HD, GROUP * HALF),
        buf(2, GROUP * HALF, HD), buf(2, HD, GROUP * HALF),
        wide(2, 1, GROUP * HALF), wide(2, 1, GROUP * HALF), wide(2, HD, GROUP * HALF),
        wide(2, 1, GROUP * HALF), wide(2, 1, GROUP * HALF), wide(2, HD, GROUP * HALF), wide(2, KB, HD), pltpu.VMEM((KB, GROUP * HALF), jnp.int32),
        buf(2, NZ, NY, 2, *half), buf(NY, NZ, *half), buf(NZ, NY, *half), buf(NY, NZ, *half), buf(NZ, NY, *half),
        buf(2, 4, *half), buf(2, NZ, *half), buf(2, 1, HALF, HD), buf(3, 2, *half),
        buf(2, 1, HALF, HD), buf(2, *half), buf(2, 2, *half), buf(3, 2, NY, *half),
        buf(2, ROWS, HD),
        pltpu.SemaphoreType.DMA((160,)), pltpu.SemaphoreType.DMA((160,)), pltpu.SemaphoreType.DMA((16,)),
    ]
    rows = jax.ShapeDtypeStruct((OWN, D), BF16)
    return tuple(
        pl.pallas_call(
            kernel,
            out_shape=[rows, rows],
            in_specs=[here] * 2 + [there] * 10,
            out_specs=[here] * 2,
            scratch_shapes=scratch,
            compiler_params=pltpu.CompilerParams(
                collective_id=1, has_side_effects=True, vmem_limit_bytes=VMEM
            ),
            cost_estimate=pl.CostEstimate(flops=10**10, bytes_accessed=1 << 24, transcendentals=0),
        )(
            patch_lengths, norm_gain.reshape(1, D), byte_rows, pool_query, pool_key, pool_value, pool_out,
            query_weight, key_weight, value_weight, out_weight, cotangent,
        )
    )


def solution(mesh):
    placed = (
        P("seq", None),
        P("seq", None),
        P(None, "tensor"),
        P(None, "tensor"),
        P(None, "tensor"),
        P("tensor", None),
        P(),
        P("seq", "tensor"),
        P(None, "tensor"),
        P(None, "tensor"),
        P("tensor", None),
        P(("seq", "tensor"), None),
    )
    return jax.shard_map(
        on_device,
        mesh=mesh,
        in_specs=placed,
        out_specs=(P(("seq", "tensor"), None), P(("seq", "tensor"), None)),
        check_vma=False,
    )
```

time: 759 us -> 152 us (0.20)
  waiting for transfers between devices: 315 us -> 0 us
  matrix products: 183 us -> 0 us
  Pallas kernels: 0 us -> 145 us
  blocking collectives: 104 us -> 0 us
  local copies, waits for them, and re-layouts: 99.3 us -> 4.65 us
  other arithmetic: 29.6 us -> 0 us
  between operations: 14.5 us -> 0.64 us
    all_gather x7 -> x0, waiting for transfers between devices: 235 us -> none  [the longest x1 75.2 us: on_device(): query_full = lax.all_gather(query_weight, 'seq', axis=0, tiled=True)]
    dot_general x70 -> x0, matrix products: 183 us -> none  [the longest x24 65.8 us: head_scores(): jnp.einsum('gqd,kd->gqk', q_heads, key_block, preferred_element_type=jnp....]
    pallas_call x0 -> x1, Pallas kernels: none -> 145 us  [on_device(): pl.pallas_call(kernel, out_shape=[rows, rows], in_specs=[here] * 2 + [the...]
    all_gather x2 -> x0, blocking collectives: 104 us -> none  [the longest x1 52.3 us: on_device(): lax.all_gather(delta, 'seq', axis=1, tiled=True)]
    reduce_scatter x3 -> x0, waiting for transfers between devices: 78.8 us -> none  [the longest x1 33.4 us: on_device(): lax.psum_scatter(partial_value, 'tensor', scatter_dimension=0, tiled=True)]
    dynamic_slice x40 -> x0, local copies, waits for them, and re-layouts: 66.4 us -> none  [the longest x16 39.2 us: step(): g_rows = lax.dynamic_slice_in_dim(g_piece, at, sub, 0)]
    reshape x17 -> x1, local copies, waits for them, and re-layouts: 27.4 us -> 1.31 us  [on_device(): norm_gain.reshape(1, D)]
    reduce_sum x11 -> x0, other arithmetic: 18.9 us -> none  [the longest x8 16.4 us: max_pass(): jnp.sum(jnp.exp(scores - new_top[..., None]), -1)]
  transfers between devices with their start and end apart: 10 -> 0, of which waited for: 8 -> 0; matrix products, arithmetic and copies ran while one was open for 17% -> 0% of each run, Pallas kernels for 0% -> 0%
where the time goes in v2:
time: 152 us; the launch traced here: 150 us
  Pallas kernels  145 us (95%)
  local copies, waits for them, and re-layouts  4.65 us (3%)
    pallas_call x1, Pallas kernels, on_device(): pl.pallas_call(kernel, out_shape=[rows, rows], in_specs=[here] * 2 + [the...  145 us
    unnamed x2, local copies, waits for them, and re-layouts  3.34 us

profile of v2, /device:TPU:2, one launch (start us, length us, event | category | flops | bytes accessed | tf_op | source)
XLA Modules:
  0.0 150.3 jit_solution(8250333803945545484)
XLA Ops:
  0.6 1.3 reshape.7.gain
  1.9 145.0 %shard_map.131 = (bf16[32,4096]{1,0:T(8,128)(2,1)}, bf16[32,4096]{1,0:T(8,128)(2,1)}) custom-call(s32[1,128]{1,0:T(1,128)} %lengths.1, bf16[1,4096]{1,0:T(2,128)(2,1)} %reshape.7.gain, bf16[512,1024]{1,0:T(8,128)(2,1)} %byte_h.1, bf16[1024,256]{1,0:T(8,128)(2,1)} %pq_h.1, bf16[1024,256]{1,0:T(8,128)(2,1)} %pk_h.1, bf16[1024,256]{1,0:T(8,128)(2,1)} %pv_h.1, ...), custom_call_target="tpu_custom_call" | custom-call | flops 10000000000 | bytes 16777216 | tf_op jit(solution)/shard_map/pallas_call | solution.py:707
  147.0 1.7 %copy.16 = bf16[32,4096]{1,0:T(8,128)(2,1)} copy(bf16[32,4096]{1,0:T(8,128)(2,1)} %get-tuple-element.4) | data formatting | bytes 524288
  148.7 1.7 %copy.17 = bf16[32,4096]{1,0:T(8,128)(2,1)} copy(bf16[32,4096]{1,0:T(8,128)(2,1)} %get-tuple-element.5) | data formatting | bytes 524288

commit v3 on v2

--- a/solution.py
+++ b/solution.py
@@ -47,6 +47,7 @@
         self.down = self.seq(self.zz(-1), self.y, self.c)
         self.north = self.seq(self.z, self.yy(1), self.c)
         self.south = self.seq(self.z, self.yy(-1), self.c)
+        self.across = self.seq(self.z, self.yy(2), self.c)
         self.twin = SHARDS - 1 - s
 
     def zz(self, i):
@@ -93,7 +94,7 @@
 
 
 def partners(at):
-    ring = [{"seq": d} for d in (at.sib, at.up, at.down, at.north, at.south, at.twin)]
+    ring = [{"seq": d} for d in (at.sib, at.up, at.down, at.north, at.south, at.across, at.twin)]
     return ring + [{"tensor": at.tt(1)}, {"tensor": at.tt(-1)}]
 
 
@@ -114,73 +115,122 @@
     return net.put(view, view, **device)
 
 
-def gather_zy(net, at, buf):
-    rows = buf.shape[4] // 2
-    zz, yy, c, y = at.zz, at.yy, at.c, at.y
-    for i in range(1, 4):
-        p = same(net, buf.at[0, zz(1 - i), y, c], seq=at.up)
-        m = same(net, buf.at[0, zz(i - 1), y, c], seq=at.down)
-        yield
-        p.wait_recv()
-        m.wait_recv()
-    p = same(net, buf.at[0, zz(-3), y, c, pl.ds(0, rows)], seq=at.up)
-    m = same(net, buf.at[0, zz(3), y, c, pl.ds(rows, rows)], seq=at.down)
-    yield
-    p.wait_recv()
-    m.wait_recv()
-    every = pl.ds(0, NZ)
-    p = same(net, buf.at[0, every, y, c], seq=at.north)
-    m = same(net, buf.at[0, every, y, c], seq=at.south)
-    sib = [same(net, buf.at[0, every, y, c], seq=at.sib)]
-    yield
-    p.wait_recv()
-    m.wait_recv()
-    p = same(net, buf.at[0, pl.ds(0, 4), yy(-1), c], seq=at.north)
-    m = same(net, buf.at[0, pl.ds(4, 4), yy(1), c], seq=at.south)
-    sib.append(same(net, buf.at[0, every, yy(-1), c], seq=at.sib))
-    sib.append(same(net, buf.at[0, every, yy(1), c], seq=at.sib))
-    yield
-    p.wait_recv()
-    m.wait_recv()
-    sib.append(same(net, buf.at[0, every, yy(2), c], seq=at.sib))
-    yield
-    for copy in sib:
-        copy.wait_recv()
-
-
-def gather_yz(net, at, buf):
-    rows = buf.shape[4] // 2
-    zz, yy, c, z = at.zz, at.yy, at.c, at.z
-    p = same(net, buf.at[1, z, at.y, c], seq=at.north)
-    m = same(net, buf.at[1, z, at.y, c], seq=at.south)
+def gather(net, at, buf):
+    n = buf.shape[4] // 2
+    zz, yy, c, y, z = at.zz, at.yy, at.c, at.y, at.z
+    every, low, high = pl.ds(0, NY), pl.ds(0, n), pl.ds(n, n)
+
+    def unit(o, j):
+        return buf.at[0, zz(o), yy(j), c]
+
+    def piece(o, j, rows):
+        return buf.at[0, zz(o), yy(j), c, rows]
+
+    def z_send(i):
+        if i < 3:
+            return [same(net, unit(-i, 0), seq=at.up), same(net, unit(i, 0), seq=at.down)]
+        return [same(net, piece(-3, 0, low), seq=at.up), same(net, piece(3, 0, high), seq=at.down)]
+
+    def y_send(*offsets):
+        return [
+            same(net, unit(o, 0), seq=to) for o in offsets for to in (at.north, at.south)
+        ]
+
+    def y_pass(*offsets):
+        if len(offsets) == 1:
+            o = offsets[0]
+            return [same(net, piece(o, -1, low), seq=at.north), same(net, piece(o, 1, high), seq=at.south)]
+        o, q = offsets
+        return [same(net, unit(o, -1), seq=at.north), same(net, unit(q, 1), seq=at.south)]
+
+    def got(copies):
+        for copy in copies:
+            copy.wait_recv()
+
+    def group_send(i):
+        pairs = []
+        for k in range(2):
+            pair = pl.ds(2 * k, 2)
+            go = []
+            if i < 3 or k == 0:
+                go.append(same(net, buf.at[1, zz(-i), pair, c], seq=at.up))
+            if i < 3 or k == 1:
+                go.append(same(net, buf.at[1, zz(i), pair, c], seq=at.down))
+            pairs.append(go)
+        return pairs
+
+    def group_pass(i, pairs):
+        after = []
+        for k in range(2):
+            pair = pl.ds(2 * k, 2)
+            got(pairs[k])
+            go = []
+            if i < 3 or k == 0:
+                go.append(same(net, buf.at[1, zz(-i), pair, c], seq=at.up))
+            if i < 3 or k == 1:
+                go.append(same(net, buf.at[1, zz(i), pair, c], seq=at.down))
+            after.append(go)
+        return after
+
+    def share(*offsets):
+        return [same(net, buf.at[1, zz(o), every, c], seq=at.sib) for o in offsets]
+
+    def share0(j):
+        return same(net, buf.at[0, pl.ds(0, NZ), yy(j), c], seq=at.sib)
+
+    mine = buf.at[1, z, y, c]
+    first = [same(net, mine, seq=to) for to in (at.north, at.south, at.across)]
+    zs = z_send(0)
+    ys = [y_send(0)]
     yield ()
-    p.wait_recv()
-    m.wait_recv()
-    p = same(net, buf.at[1, z, yy(-1), c, pl.ds(0, rows)], seq=at.north)
-    m = same(net, buf.at[1, z, yy(1), c, pl.ds(rows, rows)], seq=at.south)
+    got(first)
+    pairs = group_send(0)
+    sib = share(0)
+    got(zs)
+    zs = z_send(1)
+    ys.append(y_send(1, -1))
     yield ()
-    p.wait_recv()
-    m.wait_recv()
-    every = pl.ds(0, NY)
-    sib, offsets = [same(net, buf.at[1, z, every, c], seq=at.sib)], (0,)
-    for i in range(1, 5):
-        if i < 4:
-            p = same(net, buf.at[1, zz(1 - i), every, c], seq=at.up)
-            m = same(net, buf.at[1, zz(i - 1), every, c], seq=at.down)
-        else:
-            p = same(net, buf.at[1, zz(-3), pl.ds(0, 2), c], seq=at.up)
-            m = same(net, buf.at[1, zz(3), pl.ds(2, 2), c], seq=at.down)
-        for copy in sib:
-            copy.wait_recv()
-        yield offsets
-        p.wait_recv()
-        m.wait_recv()
-        offsets = (i, -i) if i < 4 else (4,)
-        sib = [same(net, buf.at[1, zz(o), every, c], seq=at.sib) for o in offsets]
-    yield ()
-    for copy in sib:
-        copy.wait_recv()
-    yield offsets
+    got(zs)
+    zs = z_send(2)
+    ys.append(y_send(2, -2))
+    pairs = group_pass(1, pairs)
+    got(sib)
+    sib = share(1, -1)
+    got(ys[0])
+    passed = y_pass(0)
+    yield (0,)
+    got(zs)
+    zs = z_send(3)
+    ys.append(y_send(3, -3))
+    pairs = group_pass(2, pairs)
+    got(sib)
+    sib = share(2, -2)
+    got(ys[1])
+    passed += y_pass(1, -1)
+    yield (1, -1)
+    got(zs)
+    ys.append(y_send(4))
+    pairs = group_pass(3, pairs)
+    got(sib)
+    sib = share(3, -3)
+    sib0 = [share0(0)]
+    got(ys[2])
+    passed += y_pass(2, -2)
+    yield (2, -2)
+    got(ys[3])
+    passed += y_pass(3, -3)
+    got(pairs[0] + pairs[1])
+    got(sib)
+    sib = share(4)
+    got(ys[4])
+    passed += y_pass(4)
+    sib0 += [share0(1), share0(-1)]
+    yield (3, -3)
+    got(passed)
+    sib0.append(share0(2))
+    got(sib)
+    yield (4,)
+    got(sib0)
 
 
 def gather_x(net, at, buf, row):
@@ -224,115 +274,166 @@
     result(row, mine + second[0].astype(F32) + second[1].astype(F32))
 
 
-def scatter_yz(net, at, part, sib, acc, y_first, y_second, z_first, z_next, out):
-    yy, zz = at.yy, at.zz
-    low, high = pl.ds(0, 4), pl.ds(4, 4)
-    order = (yy(2), yy(1), yy(-1), yy(0))
-    near = [
-        net.put(part.at[0, pl.ds(0, NZ), y, 1 - at.c], sib.at[y], seq=at.sib) for y in order
+def slot(o):
+    return o % NZ
+
+
+def scatter(net, at, part, sib, acc, y_first, y_next, za_first, za_next, zb_first, zb_next, y_last, out):
+    zz, yy = at.zz, at.yy
+    both, every = pl.ds(0, 2), pl.ds(0, NY)
+    one, two = pl.ds(0, 1), pl.ds(1, 1)
+    near, firsts, nexts, ring0, ring1 = {}, {}, {}, {}, {}
+
+    def got(copies):
+        for copy in copies:
+            copy.wait_recv()
+
+    def share(offsets):
+        for o in offsets:
+            near[o] = net.put(part.at[both, zz(o), every, 1 - at.c], sib.at[both, zz(o)], seq=at.sib)
+
+    def own(offsets):
+        for o in offsets:
+            near[o].wait_recv()
+            z = zz(o)
+            acc[:, z] = (part[:, z, :, at.c].astype(F32) + sib[:, z].astype(F32)).astype(BF16)
+
+    def y_one(offsets):
+        for o in offsets:
+            src, dst = acc.at[0, zz(o), yy(2)], y_first.at[slot(o)]
+            if o in (0, 4):
+                firsts[o] = [
+                    net.put(src.at[one], dst.at[one], seq=at.north),
+                    net.put(src.at[two], dst.at[two], seq=at.south),
+                ]
+            else:
+                firsts[o] = [net.put(src, dst, seq=at.north if o > 0 else at.south)]
+
+    def y_two(offsets):
+        for o in offsets:
+            got(firsts[o])
+            z, came = zz(o), y_first.at[slot(o)]
+            if o in (0, 4):
+                add_into(acc.at[0, z, yy(1), one], came.at[one])
+                add_into(acc.at[0, z, yy(-1), two], came.at[two])
+            else:
+                add_into(acc.at[0, z, yy(1 if o > 0 else -1)], came)
+            nexts[o] = [
+                net.put(acc.at[0, z, yy(1)], y_next.at[slot(o), 0], seq=at.north),
+                net.put(acc.at[0, z, yy(-1)], y_next.at[slot(o), 1], seq=at.south),
+            ]
+
+    def y_done(offsets):
+        for o in offsets:
+            got(nexts[o])
+
+    def z_zero(i):
+        def total(o, *came):
+            add_into(acc.at[0, zz(o), at.y], y_next.at[slot(o), 0], y_next.at[slot(o), 1], *came)
+
+        if i == 4:
+            total(4)
+            src = acc.at[0, zz(4), at.y]
+            ring0[4] = [
+                net.put(src.at[one], za_first.at[one], seq=at.up),
+                net.put(src.at[two], za_first.at[two], seq=at.down),
+            ]
+            return
+        got(ring0[i + 1])
+        if i == 0:
+            block = acc[0, at.z, at.y].astype(F32)
+            for came in (y_next.at[0, 0], y_next.at[0, 1], za_next.at[0, 0], za_next.at[0, 1]):
+                block = block + came[...].astype(F32)
+            out(0, block)
+            return
+        if i == 3:
+            total(3)
+            total(-3)
+            add_into(acc.at[0, zz(3), at.y, one], za_first.at[one])
+            add_into(acc.at[0, zz(-3), at.y, two], za_first.at[two])
+        else:
+            total(i, za_next.at[i, 0])
+            total(-i, za_next.at[i, 1])
+        ring0[i] = [
+            net.put(acc.at[0, zz(i), at.y], za_next.at[i - 1, 0], seq=at.up),
+            net.put(acc.at[0, zz(-i), at.y], za_next.at[i - 1, 1], seq=at.down),
+        ]
+
+    def z_one(i):
+        low, high = pl.ds(0, 2), pl.ds(2, 2)
+        if i == 4:
+            ring1[4] = [
+                net.put(acc.at[1, zz(4), low], zb_first.at[low], seq=at.up),
+                net.put(acc.at[1, zz(4), high], zb_first.at[high], seq=at.down),
+            ]
+            return
+        if i == 3:
+            got(ring1[4])
+            add_into(acc.at[1, zz(3), low], zb_first.at[low])
+            add_into(acc.at[1, zz(-3), high], zb_first.at[high])
+        go = []
+        for k, pair in enumerate((low, high)):
+            for side, o, to in ((0, i, at.up), (1, -i, at.down)):
+                if i < 3:
+                    ring1[i + 1][2 * k + side].wait_recv()
+                    add_into(acc.at[1, zz(o), pair], zb_next.at[i, side, pair])
+                go.append(net.put(acc.at[1, zz(o), pair], zb_next.at[i - 1, side, pair], seq=to))
+        ring1[i] = go
+
+    rounds = ((4,), (3, -3), (2, -2), (1, -1), (0,))
+    yield rounds[0]
+    share(rounds[0])
+    yield rounds[1]
+    share(rounds[1])
+    own(rounds[0])
+    z_one(4)
+    y_one(rounds[0])
+    yield rounds[2]
+    share(rounds[2])
+    own(rounds[1])
+    z_one(3)
+    y_one(rounds[1])
+    y_two(rounds[0])
+    yield rounds[3]
+    share(rounds[3])
+    own(rounds[2])
+    z_one(2)
+    y_one(rounds[2])
+    y_two(rounds[1])
+    y_done(rounds[0])
+    z_zero(4)
+    yield rounds[4]
+    share(rounds[4])
+    own(rounds[3])
+    z_one(1)
+    y_one(rounds[3])
+    y_two(rounds[2])
+    y_done(rounds[1])
+    z_zero(3)
+    yield ()
+    own(rounds[4])
+    y_one(rounds[4])
+    y_two(rounds[3])
+    y_done(rounds[2])
+    z_zero(2)
+    got(ring1[1])
+    add_into(acc.at[1, at.z], zb_next.at[0, 0], zb_next.at[0, 1])
+    last = [
+        net.put(acc.at[1, at.z, yy(j)], y_last.at[k], seq=to)
+        for k, (j, to) in enumerate(((2, at.across), (1, at.north), (-1, at.south)))
     ]
-    yield
-
-    def own(k):
-        near[k].wait_recv()
-        y = order[k]
-        acc[y] = (part[0, :, y, at.c].astype(F32) + sib[y].astype(F32)).astype(BF16)
-
-    own(0)
-    p = net.put(acc.at[yy(2), low], y_first.at[0], seq=at.north)
-    m = net.put(acc.at[yy(2), high], y_first.at[1], seq=at.south)
-    own(1)
-    own(2)
-    yield
-    p.wait_recv()
-    add_into(acc.at[yy(1), low], y_first.at[0])
-    p = net.put(acc.at[yy(1)], y_second.at[0], seq=at.north)
-    m.wait_recv()
-    add_into(acc.at[yy(-1), high], y_first.at[1])
-    m = net.put(acc.at[yy(-1)], y_second.at[1], seq=at.south)
-    own(3)
-    yield
-    p.wait_recv()
-    m.wait_recv()
-    add_into(acc.at[at.y], y_second.at[0], y_second.at[1])
-    mine = acc.at[at.y]
-    low, high = pl.ds(0, 1), pl.ds(1, 1)
-    p = net.put(mine.at[zz(4), low], z_first.at[0], seq=at.up)
-    m = net.put(mine.at[zz(4), high], z_first.at[1], seq=at.down)
-    yield
-    p.wait_recv()
-    m.wait_recv()
-    add_into(mine.at[zz(3), low], z_first.at[0])
-    add_into(mine.at[zz(-3), high], z_first.at[1])
-    for i in (3, 2, 1):
-        p = net.put(mine.at[zz(i)], z_next.at[i - 1, 0], seq=at.up)
-        m = net.put(mine.at[zz(-i)], z_next.at[i - 1, 1], seq=at.down)
-        yield
-        p.wait_recv()
-        m.wait_recv()
-        if i > 1:
-            add_into(mine.at[zz(i - 1)], z_next.at[i - 1, 0])
-            add_into(mine.at[zz(1 - i)], z_next.at[i - 1, 1])
-    total = mine[at.z].astype(F32) + z_next[0, 0].astype(F32) + z_next[0, 1].astype(F32)
-    out(0, total)
-
-
-def scatter_zy(net, at, part, sib, acc, z_first, z_next, y_first, y_second, out):
-    zz, yy = at.zz, at.yy
-    every = pl.ds(0, NY)
-    low, high = pl.ds(0, 2), pl.ds(2, 2)
-
-    def share(*offsets):
-        return [
-            (o, net.put(part.at[1, zz(o), every, 1 - at.c], sib.at[zz(o)], seq=at.sib)) for o in offsets
-        ]
-
-    def own(near):
-        for o, copy in near:
-            copy.wait_recv()
-            z = zz(o)
-            acc[z] = (part[1, z, :, at.c].astype(F32) + sib[z].astype(F32)).astype(BF16)
-
-    yield (4,)
-    near = share(4)
-    yield (3, -3)
-    own(near)
-    near = share(3, -3)
-    p = net.put(acc.at[zz(4), low], z_first.at[0], seq=at.up)
-    m = net.put(acc.at[zz(4), high], z_first.at[1], seq=at.down)
-    for i in (3, 2, 1):
-        yield (i - 1, 1 - i) if i > 1 else (0,)
-        own(near)
-        near = share(i - 1, 1 - i) if i > 1 else share(0)
-        p.wait_recv()
-        m.wait_recv()
-        if i == 3:
-            add_into(acc.at[zz(3), low], z_first.at[0])
-            add_into(acc.at[zz(-3), high], z_first.at[1])
-        else:
-            add_into(acc.at[zz(i)], z_next.at[i, 0])
-            add_into(acc.at[zz(-i)], z_next.at[i, 1])
-        p = net.put(acc.at[zz(i)], z_next.at[i - 1, 0], seq=at.up)
-        m = net.put(acc.at[zz(-i)], z_next.at[i - 1, 1], seq=at.down)
     yield ()
-    own(near)
-    p.wait_recv()
-    m.wait_recv()
-    mine = acc.at[at.z]
-    add_into(mine, z_next.at[0, 0], z_next.at[0, 1])
-    p = net.put(mine.at[yy(2), pl.ds(0, 1)], y_first.at[0], seq=at.north)
-    m = net.put(mine.at[yy(2), pl.ds(1, 1)], y_first.at[1], seq=at.south)
+    y_two(rounds[4])
+    y_done(rounds[3])
+    z_zero(1)
     yield ()
-    p.wait_recv()
-    m.wait_recv()
-    add_into(mine.at[yy(1), pl.ds(0, 1)], y_first.at[0])
-    add_into(mine.at[yy(-1), pl.ds(1, 1)], y_first.at[1])
-    p = net.put(mine.at[yy(1)], y_second.at[0], seq=at.north)
-    m = net.put(mine.at[yy(-1)], y_second.at[1], seq=at.south)
-    yield ()
-    p.wait_recv()
-    m.wait_recv()
-    out(1, mine[at.y].astype(F32) + y_second[0].astype(F32) + y_second[1].astype(F32))
+    got(last)
+    block = acc[1, at.z, at.y].astype(F32)
+    for k in range(3):
+        block = block + y_last[k].astype(F32)
+    out(1, block)
+    y_done(rounds[4])
+    z_zero(0)
 
 
 def pool(lengths, byte, pool_query, pool_key, pool_value):
@@ -378,7 +479,7 @@
     part, first, second, part2, first2, second2, part3, first3, second3, grad_acc,
     acc, q, g, qb, gb, attn, dq, ob, dqb,
     kvb, qs, qt, gs, gt, top, mass, oacc, lse, delta, dqt, dkv_acc, ahead,
-    pgrad, sib0, sib1, acc0, acc1, ya1, ya2, za1, za2, yb1, yb2, zb1, zb2, dkv,
+    pgrad, sib, gsum, y1, y2, za1, za2, zb1, zb2, y3, dkv,
     send, recv, local,
 ):
     at = Place()
@@ -409,14 +510,12 @@
     greet(partners(at))
 
     ready("wq0", "wq1")
-    w0, w1 = gather_zy(net, at, wq), gather_yz(net, at, wq)
-    next(w0)
-    next(w1)
+    weights = gather(net, at, wq)
+    next(weights)
 
     ready("byte", "pq", "pk", "pv")
     pooled[...] = pool(lengths, byte, pool_q, pool_k, pool_v)
-    next(w0)
-    next(w1)
+    next(weights)
     ready("po")
     for i in range(8):
         cols = pl.ds(i * 512, 512)
@@ -433,7 +532,7 @@
         yield from scatter_x(net, at, part, 16 * k, first.at[k], second.at[k], own)
         yield from gather_x(net, at, normed, 16 * k)
 
-    run([patch_chain(0), patch_chain(1), w0, w1])
+    run([patch_chain(0), patch_chain(1), weights])
 
     def normed_cols(i):
         return normed[:, :, columns(i)].reshape(ROWS, 512)
@@ -451,9 +550,8 @@
         for which in range(2):
             block = acc[half * HALF:(half + 1) * HALF, which * HD:(which + 1) * HD]
             kvb[half, at.z, at.y, at.c, which] = block.astype(BF16)
-    k0, k1 = gather_zy(net, at, kvb), gather_yz(net, at, kvb)
-    next(k1)
-    next(k0)
+    spread = gather(net, at, kvb)
+    next(spread)
     cot_chains = [gather_x(net, at, cots, 0), gather_x(net, at, cots, 16)]
     for chain in cot_chains:
         next(chain)
@@ -467,8 +565,7 @@
 
     q[...] = acc[...].astype(BF16)
     q_swap = net.put(q.at[pl.ds(HALF, HALF)], qb, seq=at.twin)
-    next(k1)
-    next(k0)
+    next(spread)
 
     def prepare(st, block, straight, turned):
         straight[st] = stack(block)
@@ -480,8 +577,7 @@
     oacc[...] = jnp.zeros_like(oacc)
     for chain in cot_chains:
         next(chain)
-    offsets = next(k1)
-    next(k0)
+    offsets = next(spread)
     q_swap.wait_recv()
     prepare(1, qb[...], qs, qt)
 
@@ -540,24 +636,13 @@
             def _(k):
                 body(at.zz(offsets[0] * (1 - 2 * k)))
 
-    def forward_group(half, z):
-        tasks(forward, half, z)
-
-    steps = 0
+    stage = 0
     while offsets is not None:
-        groups(lambda z: forward_group(1, z), offsets)
-        if k0 is not None:
-            try:
-                next(k0)
-            except StopIteration:
-                k0 = None
-
-                @pl.loop(0, NZ)
-                def _(z):
-                    forward_group(0, z)
-        if steps == 0:
+        groups(lambda z: tasks(forward, 1, z), offsets)
+        if stage == 0:
             for chain in cot_chains:
                 next(chain, None)
+        if stage == 1:
             acc[...] = jnp.zeros_like(acc)
 
             @pl.loop(0, 8)
@@ -566,9 +651,12 @@
 
             g[...] = acc[...].astype(BF16)
             g_swap = net.put(g.at[pl.ds(HALF, HALF)], gb, seq=at.twin)
-        steps += 1
-        offsets = next(k1, None)
-    assert k0 is None
+        stage += 1
+        offsets = next(spread, None)
+
+    @pl.loop(0, NZ)
+    def _(z):
+        tasks(forward, 0, z)
 
     prepare(0, g[0:HALF, :], gs, gt)
     g_swap.wait_recv()
@@ -584,52 +672,47 @@
     o_swap = net.put(ob, attn.at[pl.ds(HALF, HALF)], seq=at.twin)
     dqt[...] = jnp.zeros_like(dqt)
 
-    def backward_group(half, z):
-        dkv_acc[...] = jnp.zeros_like(dkv_acc)
-        tasks(backward, half, z)
-        pgrad[half, z, :, :, 0] = (dkv_acc[0] * HD ** (-0.5)).astype(BF16).reshape(NY, 2, HALF, HD)
-        pgrad[half, z, :, :, 1] = dkv_acc[1].astype(BF16).reshape(NY, 2, HALF, HD)
-
-    @pl.loop(0, NZ)
-    def _(z):
-        backward_group(0, z)
+    def backward_group(z):
+        @pl.loop(0, 2)
+        def _(half):
+            dkv_acc[...] = jnp.zeros_like(dkv_acc)
+            tasks(backward, half, z)
+            pgrad[half, z, :, :, 0] = (dkv_acc[0] * HD ** (-0.5)).astype(BF16).reshape(NY, 2, HALF, HD)
+            pgrad[half, z, :, :, 1] = dkv_acc[1].astype(BF16).reshape(NY, 2, HALF, HD)
 
     def out(half, total):
         dkv[0, pl.ds(half * HALF, HALF), :] = total[0].astype(BF16)
         dkv[1, pl.ds(half * HALF, HALF), :] = total[1].astype(BF16)
 
-    r0 = scatter_yz(net, at, pgrad, sib0, acc0, ya1, ya2, za1, za2, out)
-    next(r0)
-    o_swap.wait_recv()
-
-    @pl.loop(0, 8)
-    def _(i):
-        cols = columns(i)
-        part2[:, :, cols] = mm(attn[...], wo[:, cols]).astype(BF16).reshape(NX, OWN, 512)
-
     def layer_result(row, total):
         rows = pl.ds(row, 16)
         layer[rows, :] = (patches[rows, :].astype(F32) + total).astype(BF16)
 
-    lay = [scatter_x(net, at, part2, 16 * k, first2.at[k], second2.at[k], layer_result) for k in range(2)]
-    for chain in lay:
-        next(chain)
-    r1 = scatter_zy(net, at, pgrad, sib1, acc1, zb1, zb2, yb1, yb2, out)
-    computed = 0
-    while computed < NZ:
-        offsets = next(r1)
-        groups(lambda z: backward_group(1, z), offsets)
-        computed += len(offsets)
-        next(r0, None)
+    sums = scatter(net, at, pgrad, sib, gsum, y1, y2, za1, za2, zb1, zb2, y3, out)
+    lay = []
+    for stage in range(5):
+        groups(backward_group, next(sums))
+        if stage == 1:
+            o_swap.wait_recv()
+
+            @pl.loop(0, 8)
+            def _(i):
+                cols = columns(i)
+                part2[:, :, cols] = mm(attn[...], wo[:, cols]).astype(BF16).reshape(NX, OWN, 512)
+
+            lay = [
+                scatter_x(net, at, part2, 16 * k, first2.at[k], second2.at[k], layer_result)
+                for k in range(2)
+            ]
         for chain in lay:
             next(chain, None)
+    next(sums)
 
     attn_dq = (dqt[0] * HD ** (-0.5)).T.astype(BF16)
     dq[0:HALF, :] = unstack(attn_dq)
     dqb[...] = unstack((dqt[1] * HD ** (-0.5)).T.astype(BF16))
     dq_swap = net.put(dqb, dq.at[pl.ds(HALF, HALF)], seq=at.twin)
-    next(r1)
-    next(r0, None)
+    next(sums)
     dq_swap.wait_recv()
 
     @pl.loop(0, 8)
@@ -637,7 +720,7 @@
         w = jnp.concatenate([wq[half, i, y, c] for y in range(NY) for c in range(2) for half in range(2)], 0)
         grad_acc[:, columns(i)] = dg(dq[...], w, NT)
 
-    run([r1, r0] + lay)
+    run([sums] + lay)
 
     @pl.loop(0, 8)
     def _(i):
@@ -696,11 +779,11 @@
         buf(2, GROUP * HALF, HD), buf(2, HD, GROUP * HALF),
         wide(2, 1, GROUP * HALF), wide(2, 1, GROUP * HALF), wide(2, HD, GROUP * HALF),
         wide(2, 1, GROUP * HALF), wide(2, 1, GROUP * HALF), wide(2, HD, GROUP * HALF), wide(2, KB, HD), pltpu.VMEM((KB, GROUP * HALF), jnp.int32),
-        buf(2, NZ, NY, 2, *half), buf(NY, NZ, *half), buf(NZ, NY, *half), buf(NY, NZ, *half), buf(NZ, NY, *half),
-        buf(2, 4, *half), buf(2, NZ, *half), buf(2, 1, HALF, HD), buf(3, 2, *half),
-        buf(2, 1, HALF, HD), buf(2, *half), buf(2, 2, *half), buf(3, 2, NY, *half),
+        buf(2, NZ, NY, 2, *half), buf(2, NZ, NY, *half), buf(2, NZ, NY, *half),
+        buf(NZ, *half), buf(NZ, 2, *half), buf(*half), buf(3, 2, *half),
+        buf(NY, *half), buf(3, 2, NY, *half), buf(3, *half),
         buf(2, ROWS, HD),
-        pltpu.SemaphoreType.DMA((160,)), pltpu.SemaphoreType.DMA((160,)), pltpu.SemaphoreType.DMA((16,)),
+        pltpu.SemaphoreType.DMA((288,)), pltpu.SemaphoreType.DMA((288,)), pltpu.SemaphoreType.DMA((16,)),
     ]
     rows = jax.ShapeDtypeStruct((OWN, D), BF16)
     return tuple(

time: 152 us -> 140 us (0.921)
  Pallas kernels: 145 us -> 133 us
    pallas_call x1, Pallas kernels: 145 us -> 133 us  [on_device(): pl.pallas_call(kernel, out_shape=[rows, rows], in_specs=[here] * 2 + [the...]
where the time goes in v3:
time: 140 us; the launch traced here: 138 us
  Pallas kernels  133 us (95%)
  local copies, waits for them, and re-layouts  4.65 us (3%)
    pallas_call x1, Pallas kernels, on_device(): pl.pallas_call(kernel, out_shape=[rows, rows], in_specs=[here] * 2 + [the...  133 us
    unnamed x2, local copies, waits for them, and re-layouts  3.34 us

profile of v3, /device:TPU:2, one launch (start us, length us, event | category | flops | bytes accessed | tf_op | source)
XLA Modules:
  0.0 138.5 jit_solution(6648055804360391237)
XLA Ops:
  0.6 1.3 reshape.7.gain
  1.9 133.2 %shard_map.131 = (bf16[32,4096]{1,0:T(8,128)(2,1)}, bf16[32,4096]{1,0:T(8,128)(2,1)}) custom-call(s32[1,128]{1,0:T(1,128)} %lengths.1, bf16[1,4096]{1,0:T(2,128)(2,1)} %reshape.7.gain, bf16[512,1024]{1,0:T(8,128)(2,1)} %byte_h.1, bf16[1024,256]{1,0:T(8,128)(2,1)} %pq_h.1, bf16[1024,256]{1,0:T(8,128)(2,1)} %pk_h.1, bf16[1024,256]{1,0:T(8,128)(2,1)} %pv_h.1, ...), custom_call_target="tpu_custom_call" | custom-call | flops 10000000000 | bytes 16777216 | tf_op jit(solution)/shard_map/pallas_call | solution.py:790
  135.1 1.7 %copy.16 = bf16[32,4096]{1,0:T(8,128)(2,1)} copy(bf16[32,4096]{1,0:T(8,128)(2,1)} %get-tuple-element.4) | data formatting | bytes 524288
  136.8 1.7 %copy.17 = bf16[32,4096]{1,0:T(8,128)(2,1)} copy(bf16[32,4096]{1,0:T(8,128)(2,1)} %get-tuple-element.5) | data formatting | bytes 524288

commit v4 on v3

--- a/solution.py
+++ b/solution.py
@@ -19,6 +19,7 @@
 D = 4096
 OWN = 32
 KB = 512
+SENDS, RECVS = 32, 128
 VMEM = 56 * 1024 * 1024
 F32 = jnp.float32
 BF16 = jnp.bfloat16
@@ -69,11 +70,13 @@
 
     def put(self, src, dst, **device):
         n = len(self.all)
+        if n >= SENDS:
+            self.all[n - SENDS].wait_send()
         copy = pltpu.make_async_remote_copy(
             src_ref=src,
             dst_ref=dst,
-            send_sem=self.send.at[n],
-            recv_sem=self.recv.at[n],
+            send_sem=self.send.at[n % SENDS],
+            recv_sem=self.recv.at[n % RECVS],
             device_id=device,
             device_id_type=MESH,
         )
@@ -82,7 +85,7 @@
         return copy
 
     def finish(self):
-        for copy in self.all:
+        for copy in self.all[-SENDS:]:
             copy.wait_send()
 
 
@@ -90,7 +93,7 @@
     barrier = pltpu.get_barrier_semaphore()
     for device in devices:
         pl.semaphore_signal(barrier, inc=1, device_id=device, device_id_type=MESH)
-    pl.semaphore_wait(barrier, len(devices))
+    return lambda: pl.semaphore_wait(barrier, len(devices))
 
 
 def partners(at):
@@ -115,49 +118,28 @@
     return net.put(view, view, **device)
 
 
+def got(copies):
+    for copy in copies:
+        copy.wait_recv()
+
+
 def gather(net, at, buf):
     n = buf.shape[4] // 2
     zz, yy, c, y, z = at.zz, at.yy, at.c, at.y, at.z
-    every, low, high = pl.ds(0, NY), pl.ds(0, n), pl.ds(n, n)
-
-    def unit(o, j):
-        return buf.at[0, zz(o), yy(j), c]
-
-    def piece(o, j, rows):
-        return buf.at[0, zz(o), yy(j), c, rows]
+    both, every, low, high = pl.ds(0, 2), pl.ds(0, NY), pl.ds(0, n), pl.ds(n, n)
 
     def z_send(i):
-        if i < 3:
-            return [same(net, unit(-i, 0), seq=at.up), same(net, unit(i, 0), seq=at.down)]
-        return [same(net, piece(-3, 0, low), seq=at.up), same(net, piece(3, 0, high), seq=at.down)]
-
-    def y_send(*offsets):
+        up, down = buf.at[0, zz(-i), y, c], buf.at[0, zz(i), y, c]
+        if i == 3:
+            up, down = up.at[low], down.at[high]
+        return [same(net, up, seq=at.up), same(net, down, seq=at.down)]
+
+    def y_send(half, *offsets):
         return [
-            same(net, unit(o, 0), seq=to) for o in offsets for to in (at.north, at.south)
+            same(net, buf.at[half, zz(o), y, c], seq=to)
+            for o in offsets
+            for to in (at.across, at.north, at.south)
         ]
-
-    def y_pass(*offsets):
-        if len(offsets) == 1:
-            o = offsets[0]
-            return [same(net, piece(o, -1, low), seq=at.north), same(net, piece(o, 1, high), seq=at.south)]
-        o, q = offsets
-        return [same(net, unit(o, -1), seq=at.north), same(net, unit(q, 1), seq=at.south)]
-
-    def got(copies):
-        for copy in copies:
-            copy.wait_recv()
-
-    def group_send(i):
-        pairs = []
-        for k in range(2):
-            pair = pl.ds(2 * k, 2)
-            go = []
-            if i < 3 or k == 0:
-                go.append(same(net, buf.at[1, zz(-i), pair, c], seq=at.up))
-            if i < 3 or k == 1:
-                go.append(same(net, buf.at[1, zz(i), pair, c], seq=at.down))
-            pairs.append(go)
-        return pairs
 
     def group_pass(i, pairs):
         after = []
@@ -173,64 +155,51 @@
         return after
 
     def share(*offsets):
-        return [same(net, buf.at[1, zz(o), every, c], seq=at.sib) for o in offsets]
-
-    def share0(j):
-        return same(net, buf.at[0, pl.ds(0, NZ), yy(j), c], seq=at.sib)
-
-    mine = buf.at[1, z, y, c]
-    first = [same(net, mine, seq=to) for to in (at.north, at.south, at.across)]
+        return [same(net, buf.at[both, zz(o), every, c], seq=at.sib) for o in offsets]
+
+    first = y_send(1, 0)
     zs = z_send(0)
-    ys = [y_send(0)]
+    ys = [y_send(0, 0)]
     yield ()
     got(first)
-    pairs = group_send(0)
-    sib = share(0)
+    pairs = group_pass(0, [[], []])
     got(zs)
     zs = z_send(1)
-    ys.append(y_send(1, -1))
+    ys.append(y_send(0, 1, -1))
     yield ()
     got(zs)
     zs = z_send(2)
-    ys.append(y_send(2, -2))
     pairs = group_pass(1, pairs)
+    ys.append(y_send(0, 2, -2))
+    got(ys[0])
+    sib = share(0)
+    yield ()
+    got(zs)
+    zs = z_send(3)
+    pairs = group_pass(2, pairs)
+    ys.append(y_send(0, 3, -3))
+    got(ys[1])
     got(sib)
     sib = share(1, -1)
-    got(ys[0])
-    passed = y_pass(0)
     yield (0,)
     got(zs)
-    zs = z_send(3)
-    ys.append(y_send(3, -3))
-    pairs = group_pass(2, pairs)
+    ys.append(y_send(0, 4))
+    pairs = group_pass(3, pairs)
+    got(ys[2])
     got(sib)
     sib = share(2, -2)
-    got(ys[1])
-    passed += y_pass(1, -1)
     yield (1, -1)
-    got(zs)
-    ys.append(y_send(4))
-    pairs = group_pass(3, pairs)
+    got(ys[3])
+    got(pairs[0] + pairs[1])
     got(sib)
     sib = share(3, -3)
-    sib0 = [share0(0)]
-    got(ys[2])
-    passed += y_pass(2, -2)
     yield (2, -2)
-    got(ys[3])
-    passed += y_pass(3, -3)
-    got(pairs[0] + pairs[1])
+    got(ys[4])
+    farthest = share(4)
     got(sib)
-    sib = share(4)
-    got(ys[4])
-    passed += y_pass(4)
-    sib0 += [share0(1), share0(-1)]
     yield (3, -3)
-    got(passed)
-    sib0.append(share0(2))
-    got(sib)
+    got(farthest)
     yield (4,)
-    got(sib0)
 
 
 def gather_x(net, at, buf, row):
@@ -278,15 +247,13 @@
     return o % NZ
 
 
-def scatter(net, at, part, sib, acc, y_first, y_next, za_first, za_next, zb_first, zb_next, y_last, out):
+def scatter(net, at, part, sib, acc, y_next, za_first, za_next, zb_first, zb_next, y_last, out):
     zz, yy = at.zz, at.yy
     both, every = pl.ds(0, 2), pl.ds(0, NY)
     one, two = pl.ds(0, 1), pl.ds(1, 1)
-    near, firsts, nexts, ring0, ring1 = {}, {}, {}, {}, {}
-
-    def got(copies):
-        for copy in copies:
-            copy.wait_recv()
+    low, high = pl.ds(0, 2), pl.ds(2, 2)
+    ways = ((2, at.across), (1, at.north), (-1, at.south))
+    near, ys, ring0, ring1 = {}, {}, {}, {}
 
     def share(offsets):
         for o in offsets:
@@ -298,69 +265,47 @@
             z = zz(o)
             acc[:, z] = (part[:, z, :, at.c].astype(F32) + sib[:, z].astype(F32)).astype(BF16)
 
-    def y_one(offsets):
+    def y_send(offsets):
         for o in offsets:
-            src, dst = acc.at[0, zz(o), yy(2)], y_first.at[slot(o)]
-            if o in (0, 4):
-                firsts[o] = [
-                    net.put(src.at[one], dst.at[one], seq=at.north),
-                    net.put(src.at[two], dst.at[two], seq=at.south),
-                ]
-            else:
-                firsts[o] = [net.put(src, dst, seq=at.north if o > 0 else at.south)]
-
-    def y_two(offsets):
-        for o in offsets:
-            got(firsts[o])
-            z, came = zz(o), y_first.at[slot(o)]
-            if o in (0, 4):
-                add_into(acc.at[0, z, yy(1), one], came.at[one])
-                add_into(acc.at[0, z, yy(-1), two], came.at[two])
-            else:
-                add_into(acc.at[0, z, yy(1 if o > 0 else -1)], came)
-            nexts[o] = [
-                net.put(acc.at[0, z, yy(1)], y_next.at[slot(o), 0], seq=at.north),
-                net.put(acc.at[0, z, yy(-1)], y_next.at[slot(o), 1], seq=at.south),
+            ys[o] = [
+                net.put(acc.at[0, zz(o), yy(j)], y_next.at[slot(o), k], seq=to)
+                for k, (j, to) in enumerate(ways)
             ]
 
-    def y_done(offsets):
-        for o in offsets:
-            got(nexts[o])
+    def y_sum(o, *came):
+        got(ys[o])
+        total = acc[0, zz(o), at.y].astype(F32)
+        for k in range(3):
+            total = total + y_next[slot(o), k].astype(F32)
+        for ref in came:
+            total = total + ref[...].astype(F32)
+        return total
 
     def z_zero(i):
-        def total(o, *came):
-            add_into(acc.at[0, zz(o), at.y], y_next.at[slot(o), 0], y_next.at[slot(o), 1], *came)
-
+        if i < 4:
+            got(ring0[i + 1])
+        if i == 0:
+            out(0, y_sum(0, za_next.at[0, 0], za_next.at[0, 1]))
+            return
+        for side, o in enumerate((i, -i)[:1 if i == 4 else 2]):
+            came = [za_next.at[i, side]] if i < 3 else []
+            acc[0, zz(o), at.y] = y_sum(o, *came).astype(BF16)
+        if i == 3:
+            add_into(acc.at[0, zz(3), at.y, one], za_first.at[one])
+            add_into(acc.at[0, zz(-3), at.y, two], za_first.at[two])
         if i == 4:
-            total(4)
             src = acc.at[0, zz(4), at.y]
             ring0[4] = [
                 net.put(src.at[one], za_first.at[one], seq=at.up),
                 net.put(src.at[two], za_first.at[two], seq=at.down),
             ]
             return
-        got(ring0[i + 1])
-        if i == 0:
-            block = acc[0, at.z, at.y].astype(F32)
-            for came in (y_next.at[0, 0], y_next.at[0, 1], za_next.at[0, 0], za_next.at[0, 1]):
-                block = block + came[...].astype(F32)
-            out(0, block)
-            return
-        if i == 3:
-            total(3)
-            total(-3)
-            add_into(acc.at[0, zz(3), at.y, one], za_first.at[one])
-            add_into(acc.at[0, zz(-3), at.y, two], za_first.at[two])
-        else:
-            total(i, za_next.at[i, 0])
-            total(-i, za_next.at[i, 1])
         ring0[i] = [
             net.put(acc.at[0, zz(i), at.y], za_next.at[i - 1, 0], seq=at.up),
             net.put(acc.at[0, zz(-i), at.y], za_next.at[i - 1, 1], seq=at.down),
         ]
 
     def z_one(i):
-        low, high = pl.ds(0, 2), pl.ds(2, 2)
         if i == 4:
             ring1[4] = [
                 net.put(acc.at[1, zz(4), low], zb_first.at[low], seq=at.up),
@@ -383,48 +328,20 @@
     rounds = ((4,), (3, -3), (2, -2), (1, -1), (0,))
     yield rounds[0]
     share(rounds[0])
-    yield rounds[1]
-    share(rounds[1])
-    own(rounds[0])
-    z_one(4)
-    y_one(rounds[0])
-    yield rounds[2]
-    share(rounds[2])
-    own(rounds[1])
-    z_one(3)
-    y_one(rounds[1])
-    y_two(rounds[0])
-    yield rounds[3]
-    share(rounds[3])
-    own(rounds[2])
-    z_one(2)
-    y_one(rounds[2])
-    y_two(rounds[1])
-    y_done(rounds[0])
-    z_zero(4)
-    yield rounds[4]
-    share(rounds[4])
-    own(rounds[3])
-    z_one(1)
-    y_one(rounds[3])
-    y_two(rounds[2])
-    y_done(rounds[1])
-    z_zero(3)
+    for r in range(1, 5):
+        yield rounds[r]
+        share(rounds[r])
+        own(rounds[r - 1])
+        z_one(5 - r)
+        y_send(rounds[r - 1])
+        if r > 1:
+            z_zero(6 - r)
     yield ()
     own(rounds[4])
-    y_one(rounds[4])
-    y_two(rounds[3])
-    y_done(rounds[2])
-    z_zero(2)
+    y_send(rounds[4])
     got(ring1[1])
     add_into(acc.at[1, at.z], zb_next.at[0, 0], zb_next.at[0, 1])
-    last = [
-        net.put(acc.at[1, at.z, yy(j)], y_last.at[k], seq=to)
-        for k, (j, to) in enumerate(((2, at.across), (1, at.north), (-1, at.south)))
-    ]
-    yield ()
-    y_two(rounds[4])
-    y_done(rounds[3])
+    last = [net.put(acc.at[1, at.z, yy(j)], y_last.at[k], seq=to) for k, (j, to) in enumerate(ways)]
     z_zero(1)
     yield ()
     got(last)
@@ -432,7 +349,6 @@
     for k in range(3):
         block = block + y_last[k].astype(F32)
     out(1, block)
-    y_done(rounds[4])
     z_zero(0)
 
 
@@ -475,11 +391,11 @@
 def kernel(
     lengths, gain, byte_h, pq_h, pk_h, pv_h, po_h, wq_h, wk_h, wv_h, wo_h, cot_h,
     layer, grad,
-    byte, pool_q, pool_k, pool_v, pool_o, wk, wv, wo, pooled, patches, normed, cots, wq,
+    byte, pool_q, pool_k, pool_v, pool_o, wkv, wo, pooled, patches, normed, cots, wq,
     part, first, second, part2, first2, second2, part3, first3, second3, grad_acc,
     acc, q, g, qb, gb, attn, dq, ob, dqb,
     kvb, qs, qt, gs, gt, top, mass, oacc, lse, delta, dqt, dkv_acc, ahead,
-    pgrad, sib, gsum, y1, y2, za1, za2, zb1, zb2, y3, dkv,
+    pgrad, sib, gsum, y1, za1, za2, zb1, zb2, y2, dkv,
     send, recv, local,
 ):
     at = Place()
@@ -504,47 +420,51 @@
     load("pv", pv_h, pool_v)
     load("po", po_h, pool_o)
     load("cot", cot_h, cots.at[at.t])
-    load("wk", wk_h, wk)
-    load("wv", wv_h, wv)
+    load("wk", wk_h, wkv.at[:, pl.ds(0, HD)])
+    load("wv", wv_h, wkv.at[:, pl.ds(HD, HD)])
     load("wo", wo_h, wo)
-    greet(partners(at))
-
-    ready("wq0", "wq1")
-    weights = gather(net, at, wq)
-    next(weights)
+    all_here = greet(partners(at))
 
     ready("byte", "pq", "pk", "pv")
     pooled[...] = pool(lengths, byte, pool_q, pool_k, pool_v)
-    next(weights)
     ready("po")
     for i in range(8):
         cols = pl.ds(i * 512, 512)
         part[:, :, cols] = mm(pooled[...], pool_o[:, cols]).astype(BF16).reshape(NX, OWN, 512)
+    ready("wq0", "wq1")
+    all_here()
 
     def own(row, total):
         rows = total.astype(BF16)
         patches[pl.ds(row, 16), :] = rows
         hidden = rows.astype(F32)
         inv = lax.rsqrt(jnp.mean(hidden * hidden, -1, keepdims=True) + EPS)
-        normed[at.t, pl.ds(row, 16), :] = (hidden * inv * gain[...].astype(F32)).astype(BF16)
+        normed[at.t, pl.ds(row, 16), :] = (hidden * inv * gain[...].reshape(1, D).astype(F32)).astype(BF16)
 
     def patch_chain(k):
         yield from scatter_x(net, at, part, 16 * k, first.at[k], second.at[k], own)
         yield from gather_x(net, at, normed, 16 * k)
 
-    run([patch_chain(0), patch_chain(1), weights])
+    chains = [patch_chain(0), patch_chain(1)]
+    for chain in chains:
+        next(chain)
+    weights = gather(net, at, wq)
+    next(weights)
+    for turn in range(4):
+        for chain in chains:
+            next(chain, None)
+        if turn < 3:
+            next(weights)
 
     def normed_cols(i):
         return normed[:, :, columns(i)].reshape(ROWS, 512)
 
     ready("wk", "wv", "cot", "wo")
-    acc[...] = jnp.zeros_like(acc)
+    acc[:, 0:2 * HD] = jnp.zeros((ROWS, 2 * HD), F32)
 
     @pl.loop(0, 8)
     def _(i):
-        rows = normed_cols(i)
-        acc[:, 0:HD] += mm(rows, wk[columns(i), :])
-        acc[:, HD:2 * HD] += mm(rows, wv[columns(i), :])
+        acc[:, 0:2 * HD] += mm(normed_cols(i), wkv[columns(i), :])
 
     for half in range(2):
         for which in range(2):
@@ -555,7 +475,10 @@
     cot_chains = [gather_x(net, at, cots, 0), gather_x(net, at, cots, 16)]
     for chain in cot_chains:
         next(chain)
-
+    next(weights)
+    next(weights)
+    next(spread)
+    run([weights])
     acc[...] = jnp.zeros_like(acc)
 
     @pl.loop(0, 8)
@@ -565,6 +488,8 @@
 
     q[...] = acc[...].astype(BF16)
     q_swap = net.put(q.at[pl.ds(HALF, HALF)], qb, seq=at.twin)
+    for chain in cot_chains:
+        next(chain)
     next(spread)
 
     def prepare(st, block, straight, turned):
@@ -575,8 +500,15 @@
     top[...] = jnp.full_like(top, NEG)
     mass[...] = jnp.zeros_like(mass)
     oacc[...] = jnp.zeros_like(oacc)
-    for chain in cot_chains:
-        next(chain)
+    run(cot_chains)
+    acc[...] = jnp.zeros_like(acc)
+
+    @pl.loop(0, 8)
+    def _(i):
+        acc[...] += dg(cots[:, :, columns(i)].reshape(ROWS, 512), wo[:, columns(i)], NT)
+
+    g[...] = acc[...].astype(BF16)
+    g_swap = net.put(g.at[pl.ds(HALF, HALF)], gb, seq=at.twin)
     offsets = next(spread)
     q_swap.wait_recv()
     prepare(1, qb[...], qs, qt)
@@ -636,27 +568,14 @@
             def _(k):
                 body(at.zz(offsets[0] * (1 - 2 * k)))
 
-    stage = 0
+    def forward_group(z):
+        @pl.loop(0, 2)
+        def _(half):
+            tasks(forward, half, z)
+
     while offsets is not None:
-        groups(lambda z: tasks(forward, 1, z), offsets)
-        if stage == 0:
-            for chain in cot_chains:
-                next(chain, None)
-        if stage == 1:
-            acc[...] = jnp.zeros_like(acc)
-
-            @pl.loop(0, 8)
-            def _(i):
-                acc[...] += dg(cots[:, :, columns(i)].reshape(ROWS, 512), wo[:, columns(i)], NT)
-
-            g[...] = acc[...].astype(BF16)
-            g_swap = net.put(g.at[pl.ds(HALF, HALF)], gb, seq=at.twin)
-        stage += 1
+        groups(forward_group, offsets)
         offsets = next(spread, None)
-
-    @pl.loop(0, NZ)
-    def _(z):
-        tasks(forward, 0, z)
 
     prepare(0, g[0:HALF, :], gs, gt)
     g_swap.wait_recv()
@@ -681,18 +600,17 @@
             pgrad[half, z, :, :, 1] = dkv_acc[1].astype(BF16).reshape(NY, 2, HALF, HD)
 
     def out(half, total):
-        dkv[0, pl.ds(half * HALF, HALF), :] = total[0].astype(BF16)
-        dkv[1, pl.ds(half * HALF, HALF), :] = total[1].astype(BF16)
+        dkv[half * HALF:(half + 1) * HALF, 0:HD] = total[0].astype(BF16)
+        dkv[half * HALF:(half + 1) * HALF, HD:2 * HD] = total[1].astype(BF16)
 
     def layer_result(row, total):
         rows = pl.ds(row, 16)
         layer[rows, :] = (patches[rows, :].astype(F32) + total).astype(BF16)
 
-    sums = scatter(net, at, pgrad, sib, gsum, y1, y2, za1, za2, zb1, zb2, y3, out)
-    lay = []
+    sums = scatter(net, at, pgrad, sib, gsum, y1, za1, za2, zb1, zb2, y2, out)
     for stage in range(5):
         groups(backward_group, next(sums))
-        if stage == 1:
+        if stage == 2:
             o_swap.wait_recv()
 
             @pl.loop(0, 8)
@@ -704,12 +622,12 @@
                 scatter_x(net, at, part2, 16 * k, first2.at[k], second2.at[k], layer_result)
                 for k in range(2)
             ]
-        for chain in lay:
-            next(chain, None)
+        if stage == 2 or stage == 4:
+            for chain in lay:
+                next(chain)
     next(sums)
 
-    attn_dq = (dqt[0] * HD ** (-0.5)).T.astype(BF16)
-    dq[0:HALF, :] = unstack(attn_dq)
+    dq[0:HALF, :] = unstack((dqt[0] * HD ** (-0.5)).T.astype(BF16))
     dqb[...] = unstack((dqt[1] * HD ** (-0.5)).T.astype(BF16))
     dq_swap = net.put(dqb, dq.at[pl.ds(HALF, HALF)], seq=at.twin)
     next(sums)
@@ -720,12 +638,12 @@
         w = jnp.concatenate([wq[half, i, y, c] for y in range(NY) for c in range(2) for half in range(2)], 0)
         grad_acc[:, columns(i)] = dg(dq[...], w, NT)
 
-    run([sums] + lay)
+    run([sums])
 
     @pl.loop(0, 8)
     def _(i):
         rows = columns(i)
-        total = grad_acc[:, rows] + dg(dkv[0], wk[rows, :], NT) + dg(dkv[1], wv[rows, :], NT)
+        total = grad_acc[:, rows] + dg(dkv[...], wkv[rows, :], NT)
         part3[:, :, rows] = total.astype(BF16).reshape(NX, OWN, 512)
 
     def grad_result(row, total):
@@ -733,12 +651,12 @@
         hidden = patches[rows, :].astype(F32)
         inv = lax.rsqrt(jnp.mean(hidden * hidden, -1, keepdims=True) + EPS)
         unit = hidden * inv
-        scaled = total * gain[...].astype(F32)
+        scaled = total * gain[...].reshape(1, D).astype(F32)
         mean = jnp.mean(scaled * unit, -1, keepdims=True)
         cot = cots[at.t, rows, :].astype(F32)
         grad[rows, :] = (cot + inv * (scaled - unit * mean)).astype(BF16)
 
-    run([scatter_x(net, at, part3, 16 * k, first3.at[k], second3.at[k], grad_result) for k in range(2)])
+    run([scatter_x(net, at, part3, 16 * k, first3.at[k], second3.at[k], grad_result) for k in range(2)] + lay)
     net.finish()
 
 
@@ -748,6 +666,21 @@
 
 def wide(*shape):
     return pltpu.VMEM(shape, F32)
+
+
+def finish_kernel(layer, grad, layer_out, patch_grad):
+    layer_out[...] = layer[...]
+    patch_grad[...] = grad[...]
+
+
+def finish(layer, grad):
+    here = pl.BlockSpec(memory_space=pltpu.VMEM)
+    rows = jax.ShapeDtypeStruct((OWN, D), BF16)
+    return tuple(
+        pl.pallas_call(finish_kernel, out_shape=[rows, rows], in_specs=[here] * 2, out_specs=[here] * 2)(
+            layer, grad
+        )
+    )
 
 
 def on_device(
@@ -770,7 +703,7 @@
     half = (2, HALF, HD)
     scratch = [
         buf(*byte_rows.shape), buf(*pool_query.shape), buf(*pool_key.shape), buf(*pool_value.shape),
-        buf(*pool_out.shape), buf(*key_weight.shape), buf(*value_weight.shape), buf(*out_weight.shape),
+        buf(*pool_out.shape), buf(D, 2 * HD), buf(*out_weight.shape),
         buf(ROWS, 2 * HD), buf(OWN, D), buf(NX, OWN, D), buf(NX, OWN, D), buf(2, NZ, NY, 2, 32, heads),
         *line, *line, *line, wide(ROWS, D),
         wide(ROWS, heads), buf(ROWS, heads), buf(ROWS, heads), buf(HALF, heads), buf(HALF, heads),
@@ -780,14 +713,14 @@
         wide(2, 1, GROUP * HALF), wide(2, 1, GROUP * HALF), wide(2, HD, GROUP * HALF),
         wide(2, 1, GROUP * HALF), wide(2, 1, GROUP * HALF), wide(2, HD, GROUP * HALF), wide(2, KB, HD), pltpu.VMEM((KB, GROUP * HALF), jnp.int32),
         buf(2, NZ, NY, 2, *half), buf(2, NZ, NY, *half), buf(2, NZ, NY, *half),
-        buf(NZ, *half), buf(NZ, 2, *half), buf(*half), buf(3, 2, *half),
+        buf(NZ, 3, *half), buf(*half), buf(3, 2, *half),
         buf(NY, *half), buf(3, 2, NY, *half), buf(3, *half),
-        buf(2, ROWS, HD),
-        pltpu.SemaphoreType.DMA((288,)), pltpu.SemaphoreType.DMA((288,)), pltpu.SemaphoreType.DMA((16,)),
+        buf(ROWS, 2 * HD),
+        pltpu.SemaphoreType.DMA((SENDS,)), pltpu.SemaphoreType.DMA((RECVS,)), pltpu.SemaphoreType.DMA((16,)),
     ]
     rows = jax.ShapeDtypeStruct((OWN, D), BF16)
-    return tuple(
-        pl.pallas_call(
+    return finish(
+        *pl.pallas_call(
             kernel,
             out_shape=[rows, rows],
             in_specs=[here] * 2 + [there] * 10,
@@ -798,7 +731,7 @@
             ),
             cost_estimate=pl.CostEstimate(flops=10**10, bytes_accessed=1 << 24, transcendentals=0),
         )(
-            patch_lengths, norm_gain.reshape(1, D), byte_rows, pool_query, pool_key, pool_value, pool_out,
+            patch_lengths, norm_gain, byte_rows, pool_query, pool_key, pool_value, pool_out,
             query_weight, key_weight, value_weight, out_weight, cotangent,
         )
     )

time: 140 us -> 117 us (0.84)
  Pallas kernels: 133 us -> 115 us
  local copies, waits for them, and re-layouts: 4.65 us -> 0 us
    pallas_call x1, Pallas kernels: 133 us -> 113 us  [on_device(): pl.pallas_call(kernel, out_shape=[rows, rows], in_specs=[here] * 2 + [the...]
    unnamed x2 -> x0, local copies, waits for them, and re-layouts: 3.34 us -> none
    pallas_call x0 -> x1, Pallas kernels: none -> 1.84 us  [finish(): pl.pallas_call(finish_kernel, out_shape=[rows, rows], in_specs=[here] * 2...]
where the time goes in v4:
time: 117 us; the launch traced here: 115 us
  Pallas kernels  115 us (98%)
    pallas_call x1, Pallas kernels, on_device(): pl.pallas_call(kernel, out_shape=[rows, rows], in_specs=[here] * 2 + [the...  113 us

profile of v4, /device:TPU:2, one launch (start us, length us, event | category | flops | bytes accessed | tf_op | source)
XLA Modules:
  0.0 115.2 jit_solution(2127201471848788245)
XLA Ops:
  0.6 112.8 %shard_map.131 = (bf16[32,4096]{1,0:T(8,128)(2,1)}, bf16[32,4096]{1,0:T(8,128)(2,1)}) custom-call(s32[1,128]{1,0:T(1,128)} %lengths.1, bf16[4096]{0:T(1024)(128)(2,1)} %gain.1, bf16[512,1024]{1,0:T(8,128)(2,1)} %byte_h.1, bf16[1024,256]{1,0:T(8,128)(2,1)} %pq_h.1, bf16[1024,256]{1,0:T(8,128)(2,1)} %pk_h.1, bf16[1024,256]{1,0:T(8,128)(2,1)} %pv_h.1, ...), custom_call_target="tpu_custom_call" | custom-call | flops 10000000000 | bytes 16777216 | tf_op jit(solution)/shard_map/pallas_call | solution.py:723
  113.4 1.8 %shard_map.132 = (bf16[32,4096]{1,0:T(8,128)(2,1)}, bf16[32,4096]{1,0:T(8,128)(2,1)}) custom-call(bf16[32,4096]{1,0:T(8,128)(2,1)} %get-tuple-element.4.layer, bf16[32,4096]{1,0:T(8,128)(2,1)} %get-tuple-element.5.grad), custom_call_target="tpu_custom_call" | custom-call | tf_op jit(solution)/shard_map/pallas_call | solution.py:680

commit v5 on v4

--- a/solution.py
+++ b/solution.py
@@ -44,12 +44,13 @@
         self.c = lax.rem(s, 2)
         self.t = lax.axis_index("tensor")
         self.sib = self.seq(self.z, self.y, 1 - self.c)
-        self.up = self.seq(self.zz(1), self.y, self.c)
-        self.down = self.seq(self.zz(-1), self.y, self.c)
+        self.up, self.down = self.along(1), self.along(-1)
         self.north = self.seq(self.z, self.yy(1), self.c)
         self.south = self.seq(self.z, self.yy(-1), self.c)
         self.across = self.seq(self.z, self.yy(2), self.c)
-        self.twin = SHARDS - 1 - s
+
+    def along(self, i):
+        return self.seq(self.zz(i), self.y, self.c)
 
     def zz(self, i):
         return lax.rem(self.z + NZ + i, NZ)
@@ -97,7 +98,8 @@
 
 
 def partners(at):
-    ring = [{"seq": d} for d in (at.sib, at.up, at.down, at.north, at.south, at.across, at.twin)]
+    ring = [{"seq": d} for d in (at.sib, at.up, at.down, at.north, at.south, at.across)]
+    ring += [{"seq": at.along(i)} for i in (2, -2, 3, -3, 4)]
     return ring + [{"tensor": at.tt(1)}, {"tensor": at.tt(-1)}]
 
 
@@ -167,39 +169,86 @@
     zs = z_send(1)
     ys.append(y_send(0, 1, -1))
     yield ()
+    pairs = group_pass(1, pairs)
     got(zs)
     zs = z_send(2)
-    pairs = group_pass(1, pairs)
-    ys.append(y_send(0, 2, -2))
     got(ys[0])
     sib = share(0)
+    ys.append(y_send(0, 2, -2))
     yield ()
+    pairs = group_pass(2, pairs)
     got(zs)
     zs = z_send(3)
-    pairs = group_pass(2, pairs)
+    got(ys[1])
+    last, sib = sib, share(1, -1)
     ys.append(y_send(0, 3, -3))
-    got(ys[1])
-    got(sib)
-    sib = share(1, -1)
+    got(last)
     yield (0,)
+    pairs = group_pass(3, pairs)
     got(zs)
     ys.append(y_send(0, 4))
-    pairs = group_pass(3, pairs)
     got(ys[2])
-    got(sib)
-    sib = share(2, -2)
+    last, sib = sib, share(2, -2)
+    got(last)
     yield (1, -1)
+    got(pairs[0] + pairs[1])
     got(ys[3])
-    got(pairs[0] + pairs[1])
-    got(sib)
-    sib = share(3, -3)
+    last, sib = sib, share(3, -3)
+    got(last)
     yield (2, -2)
     got(ys[4])
-    farthest = share(4)
+    last, sib = sib, share(4)
+    got(last)
+    yield (3, -3)
     got(sib)
-    yield (3, -3)
-    got(farthest)
     yield (4,)
+
+
+def gather_far(net, at, buf):
+    zz, yy, c, y, z = at.zz, at.yy, at.c, at.y, at.z
+    every, all_z = pl.ds(0, NY), pl.ds(0, NZ)
+    y_ways = (at.across, at.north, at.south)
+
+    def step(i, pairs):
+        after = []
+        for k in range(2):
+            pair = pl.ds(2 * k, 2)
+            got(pairs[k])
+            go = []
+            if i < 3 or k == 0:
+                go.append(same(net, buf.at[1, zz(-i), pair, c], seq=at.up))
+            if i < 3 or k == 1:
+                go.append(same(net, buf.at[1, zz(i), pair, c], seq=at.down))
+            after.append(go)
+        return after
+
+    def share(*offsets):
+        return [same(net, buf.at[1, zz(o), every, c], seq=at.sib) for o in offsets]
+
+    first = [same(net, buf.at[1, z, y, c], seq=to) for to in y_ways]
+    zs = [same(net, buf.at[0, z, y, c], seq=at.along(i)) for i in (1, -1, 2, -2, 3, -3, 4)]
+    yield
+    got(first)
+    pairs = step(0, [[], []])
+    got(zs)
+    ys = [same(net, buf.at[0, all_z, y, c], seq=to) for to in y_ways]
+    sib = share(0)
+    yield
+    pairs = step(1, pairs)
+    sib += share(1, -1)
+    yield
+    pairs = step(2, pairs)
+    sib += share(2, -2)
+    yield
+    pairs = step(3, pairs)
+    sib += share(3, -3)
+    got(ys)
+    sib += [same(net, buf.at[0, all_z, yy(j), c], seq=at.sib) for j in range(4)]
+    yield
+    got(pairs[0] + pairs[1])
+    sib += share(4)
+    yield
+    got(sib)
 
 
 def gather_x(net, at, buf, row):
@@ -381,7 +430,7 @@
 
 
 def unstack(value):
-    return jnp.concatenate([value[h * HALF:(h + 1) * HALF] for h in range(GROUP)], 1)
+    return jnp.concatenate([value[h * ROWS:(h + 1) * ROWS] for h in range(GROUP)], 1)
 
 
 def columns(i):
@@ -393,8 +442,8 @@
     layer, grad,
     byte, pool_q, pool_k, pool_v, pool_o, wkv, wo, pooled, patches, normed, cots, wq,
     part, first, second, part2, first2, second2, part3, first3, second3, grad_acc,
-    acc, q, g, qb, gb, attn, dq, ob, dqb,
-    kvb, qs, qt, gs, gt, top, mass, oacc, lse, delta, dqt, dkv_acc, ahead,
+    acc, attn, dq,
+    kvb, qs, qt, gs, gt, top, mass, oacc, lse, delta, dqt, ahead,
     pgrad, sib, gsum, y1, za1, za2, zb1, zb2, y2, dkv,
     send, recv, local,
 ):
@@ -419,13 +468,13 @@
     load("pk", pk_h, pool_k)
     load("pv", pv_h, pool_v)
     load("po", po_h, pool_o)
+    all_here = greet(partners(at))
+
+    ready("byte", "pq", "pk", "pv")
     load("cot", cot_h, cots.at[at.t])
     load("wk", wk_h, wkv.at[:, pl.ds(0, HD)])
     load("wv", wv_h, wkv.at[:, pl.ds(HD, HD)])
     load("wo", wo_h, wo)
-    all_here = greet(partners(at))
-
-    ready("byte", "pq", "pk", "pv")
     pooled[...] = pool(lengths, byte, pool_q, pool_k, pool_v)
     ready("po")
     for i in range(8):
@@ -448,7 +497,7 @@
     chains = [patch_chain(0), patch_chain(1)]
     for chain in chains:
         next(chain)
-    weights = gather(net, at, wq)
+    weights = gather_far(net, at, wq)
     next(weights)
     for turn in range(4):
         for chain in chains:
@@ -476,6 +525,7 @@
     for chain in cot_chains:
         next(chain)
     next(weights)
+    next(spread)
     next(weights)
     next(spread)
     run([weights])
@@ -486,78 +536,66 @@
         w = jnp.concatenate([wq[half, i, y, c] for y in range(NY) for c in range(2) for half in range(2)], 0)
         acc[...] += mm(normed_cols(i), w)
 
-    q[...] = acc[...].astype(BF16)
-    q_swap = net.put(q.at[pl.ds(HALF, HALF)], qb, seq=at.twin)
-    for chain in cot_chains:
-        next(chain)
-    next(spread)
-
-    def prepare(st, block, straight, turned):
-        straight[st] = stack(block)
-        turned[st] = straight[st].T
-
-    prepare(0, q[0:HALF, :], qs, qt)
+    def prepare(block, straight, turned):
+        straight[...] = stack(block.astype(BF16))
+        turned[...] = straight[...].T
+
+    prepare(acc[...] * c2, qs, qt)
     top[...] = jnp.full_like(top, NEG)
     mass[...] = jnp.zeros_like(mass)
     oacc[...] = jnp.zeros_like(oacc)
-    run(cot_chains)
-    acc[...] = jnp.zeros_like(acc)
-
-    @pl.loop(0, 8)
-    def _(i):
-        acc[...] += dg(cots[:, :, columns(i)].reshape(ROWS, 512), wo[:, columns(i)], NT)
-
-    g[...] = acc[...].astype(BF16)
-    g_swap = net.put(g.at[pl.ds(HALF, HALF)], gb, seq=at.twin)
+    column = lax.broadcasted_iota(jnp.int32, (KB, GROUP * ROWS), 1)
+    key = lax.broadcasted_iota(jnp.int32, (KB, GROUP * ROWS), 0)
+    ahead[...] = (key >> 6) * ROWS + (key & (HALF - 1)) - (column & (ROWS - 1))
     offsets = next(spread)
-    q_swap.wait_recv()
-    prepare(1, qb[...], qs, qt)
-
-    column = lax.broadcasted_iota(jnp.int32, (KB, GROUP * HALF), 1)
-    key = lax.broadcasted_iota(jnp.int32, (KB, GROUP * HALF), 0)
-    ahead[...] = (key >> 6) * ROWS + (key & (HALF - 1)) - (column & (HALF - 1))
 
     def keys(half, z, which):
         return kvb[half, z, :, :, which].reshape(KB, HD)
 
-    def scores(half, z, st, masked):
-        out = mm(keys(half, z, 0), qt[st]) * c2
+    def scores(half, z, masked):
+        out = mm(keys(half, z, 0), qt[...])
         if masked:
-            mine, other = lax.rem(at.s, 8) * ROWS, lax.rem(at.twin, 8) * ROWS + HALF
-            base = mine + st * (other - mine) - half * HALF
+            base = lax.rem(at.s, 8) * ROWS - half * HALF
             out = jnp.where(ahead[...] <= base, out, NEG)
         return out
 
-    def forward(half, z, st, masked):
-        out = scores(half, z, st, masked)
-        old = top[st]
-        new = jnp.maximum(old, jnp.max(out, 0, keepdims=True))
+    def forward(z, masked):
+        outs = [scores(half, z, masked) for half in range(2)]
+        old = top[...]
+        new = jnp.maximum(old, jnp.max(jnp.maximum(*outs), 0, keepdims=True))
         fade = jnp.exp2(old - new)
-        p = jnp.exp2(out - new)
-        mass[st] = mass[st] * fade + jnp.sum(p, 0, keepdims=True)
-        oacc[st] = oacc[st] * fade + dg(keys(half, z, 1), p.astype(BF16), TN)
-        top[st] = new
-
-    def backward(half, z, st, masked):
-        prob = jnp.exp2(scores(half, z, st, masked) - lse[st])
-        dprob = mm(keys(half, z, 1), gt[st])
-        ds = (prob * (dprob - delta[st])).astype(BF16)
-        dkv_acc[0] += mm(ds, qs[st])
-        dkv_acc[1] += mm(prob.astype(BF16), gs[st])
-        dqt[st] += dg(keys(half, z, 0), ds, TN)
-
-    def tasks(body, half, z):
-        @pl.loop(0, 2)
-        def _(st):
-            last = at.z + st * (NZ - 1 - 2 * at.z)
-
-            @pl.when(z < last)
+        ps = [jnp.exp2(out - new) for out in outs]
+        mass[...] = mass[...] * fade + jnp.sum(ps[0] + ps[1], 0, keepdims=True)
+        products = [dg(keys(half, z, 1), ps[half].astype(BF16), TN) for half in range(2)]
+        oacc[...] = oacc[...] * fade + products[0] + products[1]
+        top[...] = new
+
+    def store_grads(half, z, grad_k, grad_v):
+        pgrad[half, z, :, :, 0] = grad_k.astype(BF16).reshape(NY, 2, HALF, HD)
+        pgrad[half, z, :, :, 1] = grad_v.astype(BF16).reshape(NY, 2, HALF, HD)
+
+    def backward(z, masked):
+        for half in range(2):
+            prob = jnp.exp2(scores(half, z, masked) - lse[...])
+            dprob = mm(keys(half, z, 1), gt[...])
+            ds = (prob * (dprob - delta[...])).astype(BF16)
+            store_grads(half, z, mm(ds, qs[...]) * math.log(2), mm(prob.astype(BF16), gs[...]))
+            dqt[...] += dg(keys(half, z, 0), ds, TN)
+
+    def tasks(body, z, otherwise=None):
+        @pl.when(z < at.z)
+        def _():
+            body(z, False)
+
+        @pl.when(z == at.z)
+        def _():
+            body(z, True)
+
+        if otherwise is not None:
+
+            @pl.when(z > at.z)
             def _():
-                body(half, z, st, False)
-
-            @pl.when(z == last)
-            def _():
-                body(half, z, st, True)
+                otherwise(z)
 
     def groups(body, offsets):
         if len(offsets) == 1:
@@ -568,36 +606,33 @@
             def _(k):
                 body(at.zz(offsets[0] * (1 - 2 * k)))
 
-    def forward_group(z):
-        @pl.loop(0, 2)
-        def _(half):
-            tasks(forward, half, z)
-
+    stage = 0
     while offsets is not None:
-        groups(forward_group, offsets)
+        groups(lambda z: tasks(forward, z), offsets)
+        if stage == 0 or stage == 2:
+            for chain in cot_chains:
+                next(chain, None)
+        if stage == 2:
+            acc[...] = jnp.zeros_like(acc)
+
+            @pl.loop(0, 8)
+            def _(i):
+                acc[...] += dg(cots[:, :, columns(i)].reshape(ROWS, 512), wo[:, columns(i)], NT)
+
+            prepare(acc[...], gs, gt)
+        stage += 1
         offsets = next(spread, None)
 
-    prepare(0, g[0:HALF, :], gs, gt)
-    g_swap.wait_recv()
-    prepare(1, gb[...], gs, gt)
-    for st in range(2):
-        ot = (oacc[st] / mass[st]).astype(BF16)
-        lse[st] = top[st] + jnp.log2(mass[st])
-        delta[st] = jnp.sum(gt[st].astype(F32) * ot.astype(F32), 0, keepdims=True)
-        if st == 0:
-            attn[0:HALF, :] = unstack(ot.T)
-        else:
-            ob[...] = unstack(ot.T)
-    o_swap = net.put(ob, attn.at[pl.ds(HALF, HALF)], seq=at.twin)
+    ot = (oacc[...] / mass[...]).astype(BF16)
+    lse[...] = top[...] + jnp.log2(mass[...])
+    delta[...] = jnp.sum(gt[...].astype(F32) * ot.astype(F32), 0, keepdims=True)
+    attn[...] = unstack(ot.T)
     dqt[...] = jnp.zeros_like(dqt)
 
-    def backward_group(z):
-        @pl.loop(0, 2)
-        def _(half):
-            dkv_acc[...] = jnp.zeros_like(dkv_acc)
-            tasks(backward, half, z)
-            pgrad[half, z, :, :, 0] = (dkv_acc[0] * HD ** (-0.5)).astype(BF16).reshape(NY, 2, HALF, HD)
-            pgrad[half, z, :, :, 1] = dkv_acc[1].astype(BF16).reshape(NY, 2, HALF, HD)
+    def nothing(z):
+        zeros = jnp.zeros((KB, HD), F32)
+        for half in range(2):
+            store_grads(half, z, zeros, zeros)
 
     def out(half, total):
         dkv[half * HALF:(half + 1) * HALF, 0:HD] = total[0].astype(BF16)
@@ -609,9 +644,8 @@
 
     sums = scatter(net, at, pgrad, sib, gsum, y1, za1, za2, zb1, zb2, y2, out)
     for stage in range(5):
-        groups(backward_group, next(sums))
+        groups(lambda z: tasks(backward, z, nothing), next(sums))
         if stage == 2:
-            o_swap.wait_recv()
 
             @pl.loop(0, 8)
             def _(i):
@@ -627,11 +661,8 @@
                 next(chain)
     next(sums)
 
-    dq[0:HALF, :] = unstack((dqt[0] * HD ** (-0.5)).T.astype(BF16))
-    dqb[...] = unstack((dqt[1] * HD ** (-0.5)).T.astype(BF16))
-    dq_swap = net.put(dqb, dq.at[pl.ds(HALF, HALF)], seq=at.twin)
+    dq[...] = unstack((dqt[...] * HD ** (-0.5)).T.astype(BF16))
     next(sums)
-    dq_swap.wait_recv()
 
     @pl.loop(0, 8)
     def _(i):
@@ -706,12 +737,10 @@
         buf(*pool_out.shape), buf(D, 2 * HD), buf(*out_weight.shape),
         buf(ROWS, 2 * HD), buf(OWN, D), buf(NX, OWN, D), buf(NX, OWN, D), buf(2, NZ, NY, 2, 32, heads),
         *line, *line, *line, wide(ROWS, D),
-        wide(ROWS, heads), buf(ROWS, heads), buf(ROWS, heads), buf(HALF, heads), buf(HALF, heads),
-        buf(ROWS, heads), buf(ROWS, heads), buf(HALF, heads), buf(HALF, heads),
-        buf(2, NZ, NY, 2, *half), buf(2, GROUP * HALF, HD), buf(2, HD, GROUP * HALF),
-        buf(2, GROUP * HALF, HD), buf(2, HD, GROUP * HALF),
-        wide(2, 1, GROUP * HALF), wide(2, 1, GROUP * HALF), wide(2, HD, GROUP * HALF),
-        wide(2, 1, GROUP * HALF), wide(2, 1, GROUP * HALF), wide(2, HD, GROUP * HALF), wide(2, KB, HD), pltpu.VMEM((KB, GROUP * HALF), jnp.int32),
+        wide(ROWS, heads), buf(ROWS, heads), buf(ROWS, heads),
+        buf(2, NZ, NY, 2, *half), buf(heads, HD), buf(HD, heads), buf(heads, HD), buf(HD, heads),
+        wide(1, heads), wide(1, heads), wide(HD, heads),
+        wide(1, heads), wide(1, heads), wide(HD, heads), pltpu.VMEM((KB, heads), jnp.int32),
         buf(2, NZ, NY, 2, *half), buf(2, NZ, NY, *half), buf(2, NZ, NY, *half),
         buf(NZ, 3, *half), buf(*half), buf(3, 2, *half),
         buf(NY, *half), buf(3, 2, NY, *half), buf(3, *half),

time: 117 us -> 108 us (0.923); the launches traced: 115 us -> 108 us
  Pallas kernels: 115 us -> 108 us
    pallas_call x1, Pallas kernels: 113 us -> 106 us  [on_device(): pl.pallas_call(kernel, out_shape=[rows, rows], in_specs=[here] * 2 + [the...]
where the time goes in v5:
time: 108 us
  Pallas kernels  108 us (100%)
    pallas_call x1, Pallas kernels, on_device(): pl.pallas_call(kernel, out_shape=[rows, rows], in_specs=[here] * 2 + [the...  106 us

profile of v5, /device:TPU:2, one launch (start us, length us, event | category | flops | bytes accessed | tf_op | source)
XLA Modules:
  0.0 108.3 jit_solution(4026891659158765180)
XLA Ops:
  0.6 105.8 %shard_map.131 = (bf16[32,4096]{1,0:T(8,128)(2,1)}, bf16[32,4096]{1,0:T(8,128)(2,1)}) custom-call(s32[1,128]{1,0:T(1,128)} %lengths.1, bf16[4096]{0:T(1024)(128)(2,1)} %gain.1, bf16[512,1024]{1,0:T(8,128)(2,1)} %byte_h.1, bf16[1024,256]{1,0:T(8,128)(2,1)} %pq_h.1, bf16[1024,256]{1,0:T(8,128)(2,1)} %pk_h.1, bf16[1024,256]{1,0:T(8,128)(2,1)} %pv_h.1, ...), custom_call_target="tpu_custom_call" | custom-call | flops 10000000000 | bytes 16777216 | tf_op jit(solution)/shard_map/pallas_call | solution.py:752
  106.4 1.8 %shard_map.132 = (bf16[32,4096]{1,0:T(8,128)(2,1)}, bf16[32,4096]{1,0:T(8,128)(2,1)}) custom-call(bf16[32,4096]{1,0:T(8,128)(2,1)} %get-tuple-element.4.layer, bf16[32,4096]{1,0:T(8,128)(2,1)} %get-tuple-element.5.grad), custom_call_target="tpu_custom_call" | custom-call | tf_op jit(solution)/shard_map/pallas_call | solution.py:711

commit v6 on v5

--- a/solution.py
+++ b/solution.py
@@ -143,40 +143,39 @@
             for to in (at.across, at.north, at.south)
         ]
 
-    def group_pass(i, pairs):
+    def step(i, flows, units=range(4)):
         after = []
-        for k in range(2):
-            pair = pl.ds(2 * k, 2)
-            got(pairs[k])
-            go = []
-            if i < 3 or k == 0:
-                go.append(same(net, buf.at[1, zz(-i), pair, c], seq=at.up))
-            if i < 3 or k == 1:
-                go.append(same(net, buf.at[1, zz(i), pair, c], seq=at.down))
+        for k, flow in zip(units, flows):
+            got(flow)
+            j, go = (0, -1, 1, 2)[k], []
+            if i < 3 or k < 2:
+                go.append(same(net, buf.at[1, zz(-i), yy(j), c], seq=at.up))
+            if i < 3 or k >= 2:
+                go.append(same(net, buf.at[1, zz(i), yy(j), c], seq=at.down))
             after.append(go)
         return after
 
     def share(*offsets):
         return [same(net, buf.at[both, zz(o), every, c], seq=at.sib) for o in offsets]
 
-    first = y_send(1, 0)
+    across, north, south = y_send(1, 0)
+    flows = step(0, [[]], (0,))
     zs = z_send(0)
     ys = [y_send(0, 0)]
     yield ()
-    got(first)
-    pairs = group_pass(0, [[], []])
+    flows += step(0, [[north], [south], [across]], (1, 2, 3))
     got(zs)
     zs = z_send(1)
     ys.append(y_send(0, 1, -1))
     yield ()
-    pairs = group_pass(1, pairs)
+    flows = step(1, flows)
     got(zs)
     zs = z_send(2)
     got(ys[0])
     sib = share(0)
     ys.append(y_send(0, 2, -2))
     yield ()
-    pairs = group_pass(2, pairs)
+    flows = step(2, flows)
     got(zs)
     zs = z_send(3)
     got(ys[1])
@@ -184,14 +183,14 @@
     ys.append(y_send(0, 3, -3))
     got(last)
     yield (0,)
-    pairs = group_pass(3, pairs)
+    flows = step(3, flows)
     got(zs)
     ys.append(y_send(0, 4))
     got(ys[2])
     last, sib = sib, share(2, -2)
     got(last)
     yield (1, -1)
-    got(pairs[0] + pairs[1])
+    got(sum(flows, []))
     got(ys[3])
     last, sib = sib, share(3, -3)
     got(last)
@@ -266,17 +265,19 @@
     m.wait_recv()
 
 
-def add_into(ref, *others):
-    total = ref[...].astype(F32)
-    for other in others:
-        total = total + other[...].astype(F32)
-    ref[...] = total.astype(BF16)
+def add_into(ref, other):
+    ref[...] = ref[...] + other[...]
+
+
+def add_two(ref, one, two):
+    ref[...] = (ref[...].astype(F32) + one[...].astype(F32) + two[...].astype(F32)).astype(BF16)
 
 
 def scatter_x(net, at, part, row, first, second, result):
     tt = at.tt
     rows, low, high = pl.ds(row, 16), pl.ds(0, D // 2), pl.ds(D // 2, D // 2)
     p = net.put(part.at[tt(2), rows, low], first.at[0], tensor=tt(1))
+    yield
     m = net.put(part.at[tt(2), rows, high], first.at[1], tensor=tt(-1))
     yield
     p.wait_recv()
@@ -312,7 +313,7 @@
         for o in offsets:
             near[o].wait_recv()
             z = zz(o)
-            acc[:, z] = (part[:, z, :, at.c].astype(F32) + sib[:, z].astype(F32)).astype(BF16)
+            acc[:, z] = part[:, z, :, at.c] + sib[:, z]
 
     def y_send(offsets):
         for o in offsets:
@@ -389,7 +390,7 @@
     own(rounds[4])
     y_send(rounds[4])
     got(ring1[1])
-    add_into(acc.at[1, at.z], zb_next.at[0, 0], zb_next.at[0, 1])
+    add_two(acc.at[1, at.z], zb_next.at[0, 0], zb_next.at[0, 1])
     last = [net.put(acc.at[1, at.z, yy(j)], y_last.at[k], seq=to) for k, (j, to) in enumerate(ways)]
     z_zero(1)
     yield ()
@@ -462,7 +463,7 @@
             loads[name].wait()
 
     for half in range(2):
-        load("wq%d" % half, wq_h.at[pl.ds(half * 32, 32)], wq.at[half, at.z, at.y, at.c])
+        load("wq%d" % half, wq_h.at[:, pl.ds(half * 256, 256)], wq.at[half, at.z, at.y, at.c])
     load("byte", byte_h, byte)
     load("pq", pq_h, pool_q)
     load("pk", pk_h, pool_k)
@@ -496,6 +497,7 @@
 
     chains = [patch_chain(0), patch_chain(1)]
     for chain in chains:
+        next(chain)
         next(chain)
     weights = gather_far(net, at, wq)
     next(weights)
@@ -528,13 +530,15 @@
     next(spread)
     next(weights)
     next(spread)
+    for chain in cot_chains:
+        next(chain)
     run([weights])
     acc[...] = jnp.zeros_like(acc)
 
     @pl.loop(0, 8)
     def _(i):
-        w = jnp.concatenate([wq[half, i, y, c] for y in range(NY) for c in range(2) for half in range(2)], 0)
-        acc[...] += mm(normed_cols(i), w)
+        for half in range(2):
+            acc[:, half * 256:(half + 1) * 256] += mm(normed_cols(i), wq[half, i].reshape(512, 256))
 
     def prepare(block, straight, turned):
         straight[...] = stack(block.astype(BF16))
@@ -609,10 +613,8 @@
     stage = 0
     while offsets is not None:
         groups(lambda z: tasks(forward, z), offsets)
-        if stage == 0 or stage == 2:
-            for chain in cot_chains:
-                next(chain, None)
-        if stage == 2:
+        if stage == 0:
+            run(cot_chains)
             acc[...] = jnp.zeros_like(acc)
 
             @pl.loop(0, 8)
@@ -656,23 +658,27 @@
                 scatter_x(net, at, part2, 16 * k, first2.at[k], second2.at[k], layer_result)
                 for k in range(2)
             ]
-        if stage == 2 or stage == 4:
+            for chain in lay:
+                next(chain)
+                next(chain)
+        if stage == 4:
             for chain in lay:
                 next(chain)
     next(sums)
 
     dq[...] = unstack((dqt[...] * HD ** (-0.5)).T.astype(BF16))
+
+    def dq_product(i):
+        grad_acc[:, columns(i)] = dg(dq[:, 0:256], wq[0, i].reshape(512, 256), NT) + dg(
+            dq[:, 256:512], wq[1, i].reshape(512, 256), NT
+        )
+
+    pl.loop(0, 4)(dq_product)
     next(sums)
-
-    @pl.loop(0, 8)
-    def _(i):
-        w = jnp.concatenate([wq[half, i, y, c] for y in range(NY) for c in range(2) for half in range(2)], 0)
-        grad_acc[:, columns(i)] = dg(dq[...], w, NT)
-
+    pl.loop(4, 8)(dq_product)
     run([sums])
 
-    @pl.loop(0, 8)
-    def _(i):
+    def dkv_product(i):
         rows = columns(i)
         total = grad_acc[:, rows] + dg(dkv[...], wkv[rows, :], NT)
         part3[:, :, rows] = total.astype(BF16).reshape(NX, OWN, 512)
@@ -687,7 +693,12 @@
         cot = cots[at.t, rows, :].astype(F32)
         grad[rows, :] = (cot + inv * (scaled - unit * mean)).astype(BF16)
 
-    run([scatter_x(net, at, part3, 16 * k, first3.at[k], second3.at[k], grad_result) for k in range(2)] + lay)
+    chains = [scatter_x(net, at, part3, 16 * k, first3.at[k], second3.at[k], grad_result) for k in range(2)]
+    pl.loop(0, 4)(dkv_product)
+    for chain in chains:
+        next(chain)
+    pl.loop(4, 8)(dkv_product)
+    run(chains + lay)
     net.finish()
 
 
@@ -735,7 +746,7 @@
     scratch = [
         buf(*byte_rows.shape), buf(*pool_query.shape), buf(*pool_key.shape), buf(*pool_value.shape),
         buf(*pool_out.shape), buf(D, 2 * HD), buf(*out_weight.shape),
-        buf(ROWS, 2 * HD), buf(OWN, D), buf(NX, OWN, D), buf(NX, OWN, D), buf(2, NZ, NY, 2, 32, heads),
+        buf(ROWS, 2 * HD), buf(OWN, D), buf(NX, OWN, D), buf(NX, OWN, D), buf(2, NZ, NY, 2, 64, heads // 2),
         *line, *line, *line, wide(ROWS, D),
         wide(ROWS, heads), buf(ROWS, heads), buf(ROWS, heads),
         buf(2, NZ, NY, 2, *half), buf(heads, HD), buf(HD, heads), buf(heads, HD), buf(HD, heads),

time: 108 us -> 105 us (0.972); the launches traced: 108 us -> 104 us
  Pallas kernels: 108 us -> 103 us
    pallas_call x1, Pallas kernels: 106 us -> 102 us  [on_device(): pl.pallas_call(kernel, out_shape=[rows, rows], in_specs=[here] * 2 + [the...]
where the time goes in v6:
time: 105 us; the launch traced here: 104 us
  Pallas kernels  103 us (98%)
    pallas_call x1, Pallas kernels, on_device(): pl.pallas_call(kernel, out_shape=[rows, rows], in_specs=[here] * 2 + [the...  102 us

profile of v6, /device:TPU:2, one launch (start us, length us, event | category | flops | bytes accessed | tf_op | source)
XLA Modules:
  0.0 104.1 jit_solution(17558843892108319960)
XLA Ops:
  0.6 101.6 %shard_map.131 = (bf16[32,4096]{1,0:T(8,128)(2,1)}, bf16[32,4096]{1,0:T(8,128)(2,1)}) custom-call(s32[1,128]{1,0:T(1,128)} %lengths.1, bf16[4096]{0:T(1024)(128)(2,1)} %gain.1, bf16[512,1024]{1,0:T(8,128)(2,1)} %byte_h.1, bf16[1024,256]{1,0:T(8,128)(2,1)} %pq_h.1, bf16[1024,256]{1,0:T(8,128)(2,1)} %pk_h.1, bf16[1024,256]{1,0:T(8,128)(2,1)} %pv_h.1, ...), custom_call_target="tpu_custom_call" | custom-call | flops 10000000000 | bytes 16777216 | tf_op jit(solution)/shard_map/pallas_call | solution.py:763
  102.3 1.8 %shard_map.132 = (bf16[32,4096]{1,0:T(8,128)(2,1)}, bf16[32,4096]{1,0:T(8,128)(2,1)}) custom-call(bf16[32,4096]{1,0:T(8,128)(2,1)} %get-tuple-element.4.layer, bf16[32,4096]{1,0:T(8,128)(2,1)} %get-tuple-element.5.grad), custom_call_target="tpu_custom_call" | custom-call | tf_op jit(solution)/shard_map/pallas_call | solution.py:722
